TPU v7x, 32 devices: a whole 2x2x4 slice. The times are simulated.
32 devices in a mesh: gx: 4 (over z), gy: 2 (over x), gz: 4 (over y, core).
Axes of the slice: x: 2, y: 2, z: 4, core: 2. Of those that a mesh axis runs over, the one named last changes fastest.
Arguments:
- density: float32 [16, 8, 512], P('gx', 'gy', 'gz'), may hold values from 0.5 to 2
- velocity: float32 [3, 16, 8, 512], P(None, 'gx', 'gy', 'gz'), may hold values from -3 to 3
- pressure: float32 [16, 8, 512], P('gx', 'gy', 'gz'), may hold values from 0.5 to 2
- fine_density: float32 [4, 2, 8, 8, 128], P('gx', 'gy', 'gz'), may hold values from -0.2 to 0.2
- fine_velocity: float32 [3, 4, 2, 8, 8, 128], P(None, 'gx', 'gy', 'gz'), may hold values from -3 to 3
- fine_pressure: float32 [4, 2, 8, 8, 128], P('gx', 'gy', 'gz'), may hold values from -0.2 to 0.2
- box_parent: int32 [4, 2, 8, 1], P('gx', 'gy'), may hold values from 0 to 3; in each aligned block of 2 rows (0 to 1, 2 to 3, ..., all dimensions but the last counted through in order) no two rows name the same one
- box_shift: int32 [4, 2, 8], P('gx', 'gy'), may hold values from 0 to 120
Outputs:
- coarse_state: float32 [5, 16, 8, 512], P(None, 'gx', 'gy', 'gz')
- fine_state: float32 [5, 4, 2, 8, 8, 128], P(None, 'gx', 'gy', 'gz')
Inputs may be any that keep to these rules, and one draw needn't show every extreme that they name: `box_parent`: among the 2 boxes of one owner (one aligned block), no parent is named more than 1 times, and in some blocks one parent is named exactly 1 times.
All inputs are finite; a program needn't handle non-finite values.
Results may differ from a plain program's by a relative error of at most 0.0003.
Values sent between devices are 32-bit elements; how exact they have to be, the bound alone decides.
A program may use at most 64 MiB of HBM per device.

v0:
```python
import functools

import jax
import jax.numpy as jnp
from jax import lax
from jax.experimental import pallas as pl
from jax.experimental.pallas import tpu as pltpu
from jax.sharding import PartitionSpec as P

GAMMA = 1.4
DT_COARSE = 0.05
DT_FINE = 0.025
MESH = pl.DeviceIdType.MESH
F32 = jnp.float32


def mm(a, b):
    return lax.dot_general(
        a,
        b,
        (((1,), (0,)), ((), ())),
        precision=lax.Precision.HIGHEST,
        preferred_element_type=F32,
    )


def to_conserved(q):
    rho, u, v, w, p = q
    energy = p * (1.0 / (GAMMA - 1.0)) + 0.5 * rho * (u * u + v * v + w * w)
    return [rho, rho * u, rho * v, rho * w, energy]


def to_primitive(c):
    rho, mx, my, mz, energy = c
    inv = 1.0 / rho
    u, v, w = mx * inv, my * inv, mz * inv
    p = (GAMMA - 1.0) * (energy - 0.5 * (mx * u + my * v + mz * w))
    return [rho, u, v, w, p]


def minmod(a, b):
    return jnp.maximum(jnp.minimum(a, b), 0.0) + jnp.minimum(jnp.maximum(a, b), 0.0)


def hllc(left, right):
    rl, ul, _, _, pl_ = left
    rr, ur, _, _, pr = right
    cl = jnp.sqrt(GAMMA * pl_ / rl)
    cr = jnp.sqrt(GAMMA * pr / rr)
    sl = jnp.minimum(ul - cl, ur - cr)
    sr = jnp.maximum(ul + cl, ur + cr)
    ml = rl * (sl - ul)
    mr = rr * (sr - ur)
    contact = (pr - pl_ + ml * ul - mr * ur) / (ml - mr)
    use_left = (sl >= 0.0) | (contact >= 0.0)
    rho, un, t1, t2, p = [jnp.where(use_left, a, b) for a, b in zip(left, right)]
    wave = jnp.where(use_left, sl, sr)
    mass = jnp.where(use_left, ml, mr)
    outside = (sl >= 0.0) | (jnp.logical_not(use_left) & (sr < 0.0))
    scale = 1.0 / (wave - contact)
    energy = p * (1.0 / (GAMMA - 1.0)) + 0.5 * rho * (un * un + t1 * t1 + t2 * t2)
    star_rho = mass * scale
    star_energy = ((wave - un) * energy + (contact - un) * (mass * contact + p)) * scale
    flow = rho * un
    zero = jnp.zeros_like(rho)
    f0 = flow + jnp.where(outside, zero, wave * (star_rho - rho))
    fn = flow * un + p + jnp.where(outside, zero, wave * (star_rho * contact - flow))
    fe = (energy + p) * un + jnp.where(outside, zero, wave * (star_energy - energy))
    return [f0, fn, t1 * f0, t2 * f0, fe]


TURN = ((0, 1, 2, 3, 4), (0, 2, 3, 1, 4), (0, 3, 1, 2, 4))


def stacked_flux(lefts, rights):
    sizes = [part[0].shape[0] for _, part in lefts]

    def joined(parts):
        return [jnp.concatenate([part[TURN[axis][i]] for axis, part in parts]) for i in range(5)]

    fluxes = hllc(joined(lefts), joined(rights))
    out = []
    at = 0
    for (axis, _), size in zip(lefts, sizes):
        part = [None] * 5
        for i in range(5):
            part[TURN[axis][i]] = fluxes[i][at : at + size]
        out.append(part)
        at += size
    return out


def roll(a, shift, axis):
    size = a.shape[axis]
    shift = shift % size
    return a if shift == 0 else pltpu.roll(a, shift, axis)


def coarse_tendency(q, n):
    lane = lax.broadcasted_iota(jnp.int32, (1, 8, 128), 2)
    row = lax.broadcasted_iota(jnp.int32, (1, 8, 128), 1)
    inner = (row >= 2) & (row < 6)
    ly, ry, lx, rx, lz, rz = [], [], [], [], [], []
    for f in range(5):
        a = q[f]
        jump = a[1:8] - a[0:7]
        half = 0.5 * minmod(jump[0:6], jump[1:7])
        ly.append(a[1:6] + half[0:5])
        ry.append(a[2:7] - half[1:6])
        c = a[2:6]
        jump = c - roll(c, 1, 1)
        half = 0.5 * minmod(jump, roll(jump, -1, 1))
        lx.append(roll(c + half, 1, 1))
        rx.append(c - half)
        g = n[f]
        before = roll(jnp.where(lane == 127, g, c), 1, 2)
        after = roll(jnp.where(lane == 0, g, c), -1, 2)
        half = 0.5 * minmod(c - before, after - c)
        g_before = roll(jnp.where(lane == 127, c, g), 1, 2)
        g_after = roll(jnp.where(lane == 0, c, g), -1, 2)
        g_half = 0.5 * minmod(g - g_before, g_after - g)
        up = c + half
        down = c - half
        low_left = roll(jnp.where(lane == 127, g + g_half, up), 1, 2)
        high_right = roll(jnp.where(lane == 0, g - g_half, down), -1, 2)
        lz.append(jnp.where(inner, low_left, roll(up, 4, 1)))
        rz.append(jnp.where(inner, down, roll(high_right, 4, 1)))
    fx, fy, fz = stacked_flux([(0, lx), (1, ly), (2, lz)], [(0, rx), (1, ry), (2, rz)])
    out = []
    for f in range(5):
        dx = roll(fx[f], -1, 1) - fx[f]
        dy = fy[f][1:5] - fy[f][0:4]
        dz = roll(fz[f], 4, 1) - fz[f]
        out.append(-dx - dy - dz)
    return out


def fine_tendency(q, ghosts):
    lane = lax.broadcasted_iota(jnp.int32, (1, 8, 128), 2)
    row = lax.broadcasted_iota(jnp.int32, (1, 8, 128), 1)
    firsts = (row == 0, lane < 16, lane % 16 == 0)
    lasts = (row == 7, lane >= 112, lane % 16 == 15)
    steps = ((1, 1), (16, 2), (1, 2))
    lefts, rights, end_lefts, end_rights = [], [], [], []
    for axis in range(3):
        step, dim = steps[axis]
        left, right, tops = [], [], []
        for f in range(5):
            a = q[f]
            g = ghosts[axis][f]
            before = jnp.where(firsts[axis], g, roll(a, step, dim))
            after = jnp.where(lasts[axis], g, roll(a, -step, dim))
            half = 0.5 * minmod(a - before, after - a)
            up = a + half
            left.append(jnp.where(firsts[axis], g, roll(up, step, dim)))
            right.append(a - half)
            tops.append(up)
        lefts.append((axis, left))
        rights.append((axis, right))
        end_lefts.append((axis, tops))
        end_rights.append((axis, ghosts[axis]))
    parts = stacked_flux(lefts + end_lefts, rights + end_rights)
    out = [None] * 5
    for axis in range(3):
        step, dim = steps[axis]
        for f in range(5):
            low = parts[axis][f]
            change = jnp.where(lasts[axis], parts[3 + axis][f], roll(low, -step, dim)) - low
            out[f] = -change if out[f] is None else out[f] - change
    return [2.0 * part for part in out]


def kernel(
    sizes,
    density,
    velocity,
    pressure,
    fine_density,
    fine_velocity,
    fine_pressure,
    parents,
    shifts,
    coarse_out,
    fine_out,
    ext,
    xs,
    xr,
    ys,
    yr,
    zs,
    zr,
    xs1,
    xr1,
    ys1,
    yr1,
    yf,
    sel,
    expand_t,
    expand_y,
    place,
    msg,
    got,
    mean,
    mean_got,
    laid,
    upd,
    send_sem,
    recv_sem,
):
    nx, ny, nz = sizes
    cz = 128
    gx, gy, gz = lax.axis_index("gx"), lax.axis_index("gy"), lax.axis_index("gz")
    x_up, x_dn = {"gx": lax.rem(gx + 1, nx)}, {"gx": lax.rem(gx + nx - 1, nx)}
    y_up, y_dn = {"gy": lax.rem(gy + 1, ny)}, {"gy": lax.rem(gy + ny - 1, ny)}
    column = [lax.rem(gz + d, nz) for d in range(nz)]
    z_up, z_dn = {"gz": column[1]}, {"gz": column[nz - 1]}
    started = []

    def send(src, dst, device):
        at = len(started)
        copy = pltpu.make_async_remote_copy(
            src_ref=src,
            dst_ref=dst,
            send_sem=send_sem.at[at],
            recv_sem=recv_sem.at[at],
            device_id=device,
            device_id_type=MESH,
        )
        copy.start()
        started.append(copy)
        return copy

    barrier = pltpu.get_barrier_semaphore()
    partners = [x_up, x_dn, y_up, y_dn] + [{"gz": column[d]} for d in range(1, nz)]
    for device in partners:
        pl.semaphore_signal(barrier, inc=1, device_id=device, device_id_type=MESH)

    lane1 = lax.broadcasted_iota(jnp.int32, (8, 128), 1)
    lane3 = lax.broadcasted_iota(jnp.int32, (1, 8, 128), 2)

    def pack_z(fields, at):
        packed = jnp.zeros((4, 8, 128), F32)
        for f in range(5):
            packed = jnp.where(lane3 // 4 == f, roll(fields[f], 2 + 4 * f, 2), packed)
        zs[at] = packed

    def start_halos(at):
        for f in range(5):
            xs[at, 0, f] = ext[f, 2:6, 2:4, :]
            xs[at, 1, f] = ext[f, 2:6, 4:6, :]
            ys[at, 0, f] = ext[f, 2:4, 2:6, :]
            ys[at, 1, f] = ext[f, 4:6, 2:6, :]
        if at == 0:
            pl.semaphore_wait(barrier, len(partners))
        return [
            send(xs.at[at, 1], xr.at[at, 0], x_up),
            send(xs.at[at, 0], xr.at[at, 1], x_dn),
            send(ys.at[at, 1], yr.at[at, 0], y_up),
            send(ys.at[at, 0], yr.at[at, 1], y_dn),
            send(zs.at[at], zr.at[at, 0], z_up),
            send(zs.at[at], zr.at[at, 1], z_dn),
        ]

    def take_halos(at, copies):
        for copy in copies:
            copy.wait_recv()
        for f in range(5):
            ext[f, 2:6, 0:2, :] = xr[at, 0, f]
            ext[f, 2:6, 6:8, :] = xr[at, 1, f]
            ext[f, 0:2, 2:6, :] = yr[at, 0, f]
            ext[f, 6:8, 2:6, :] = yr[at, 1, f]
        ends = jnp.where(lane3 % 4 < 2, zr[at, 0], zr[at, 1])
        return [roll(ends, 126 - 4 * f, 2) for f in range(5)]

    def start_windows(at):
        for f in range(5):
            yf[f, 0:4, :] = ext[f, 1, 2:6, :]
            yf[f, 4:8, :] = ext[f, 6, 2:6, :]
        copies = []
        for chunk in range((nz + 3) // 4):
            picked = []
            for r in range(4):
                rows = [ext[f, 2 + r] for f in range(5)] + [yf[r]]
                if r == 0:
                    rows.append(yf[4])
                picked.append(mm(jnp.concatenate(rows), sel[chunk, r]))
            for d in range(4 * chunk, min(4 * chunk + 4, nz)):
                body = jnp.zeros((48, 128), F32)
                group = lax.broadcasted_iota(jnp.int32, (48, 128), 1) // 32
                for r in range(4):
                    body = jnp.where(group == (d + r) % 4, picked[r][0:48], body)
                tail = jnp.where(lane1 // 32 == d % 4, picked[0][48:56], 0.0)
                if d == 0:
                    got[at, 0, 0:48, :] = body
                    got[at, 0, 48:56, :] = tail
                else:
                    msg[at, d - 1, 0:48, :] = body
                    msg[at, d - 1, 48:56, :] = tail
                    copies.append(send(msg.at[at, d - 1], got.at[at, d], {"gz": column[d]}))
        return copies

    def take_windows(at, copies):
        for copy in copies:
            copy.wait_recv()
        total = got[at, 0]
        for d in range(1, nz):
            total = total + roll(got[at, d], -32 * (d % 4), 1)
        inner = [total[8 * f : 8 * f + 8] for f in range(5)]
        faces = [roll(total[40:48], -32 * f, 1) for f in range(4)] + [total[48:56]]
        return inner, faces

    row2 = lax.broadcasted_iota(jnp.int32, (8, 128), 0)

    def doubled(tile, base):
        out = tile[base : base + 1]
        for k in range(1, 4):
            out = jnp.where(row2 >= 2 * k, tile[base + k : base + k + 1], out)
        return jnp.broadcast_to(out, (8, 128))

    def injected(inner, faces):
        rows = [doubled(tile, 2) for tile in inner] + list(inner)
        wide = mm(jnp.concatenate(rows), expand_t[...])
        rows = [doubled(tile, 0) for tile in faces] + [doubled(tile, 4) for tile in faces]
        sides = mm(jnp.concatenate(rows), expand_y[...])

        def both(matrix, first_row, left, right):
            return jnp.stack(
                [
                    matrix[first_row : first_row + 8, left : left + 128],
                    matrix[first_row : first_row + 8, right : right + 128],
                ]
            )

        row = lax.broadcasted_iota(jnp.int32, (1, 8, 128), 1)
        cells, in_x, in_y, in_z = [], [], [], []
        for f in range(5):
            cells.append(both(wide, 8 * f, 0, 128))
            in_z.append(both(wide, 8 * f, 256, 384))
            edge = both(wide, 40 + 8 * f, 0, 128)
            in_x.append(jnp.where(row < 4, edge[:, 1:2, :], edge[:, 6:7, :]))
            low = both(sides, 8 * f, 0, 128)
            high = both(sides, 40 + 8 * f, 0, 128)
            in_y.append(jnp.where(lane3 < 64, low, high))
        return cells, (in_x, in_y, in_z)

    ext[...] = jnp.ones(ext.shape, F32)
    for y in range(4):
        ext[0, 2 + y, 2:6, :] = density[:, y, :]
        for k in range(3):
            ext[1 + k, 2 + y, 2:6, :] = velocity[k, :, y, :]
        ext[4, 2 + y, 2:6, :] = pressure[:, y, :]
    pack_z([ext[f, 2:6] for f in range(5)], 0)
    halos = start_halos(0)

    big_row = lax.broadcasted_iota(jnp.int32, (128, 128), 0)

    def one_hot(index):
        return jnp.where(big_row == index[0:1, :], 1.0, 0.0)

    slot = lane1 % 16
    for chunk in range((nz + 3) // 4):
        target = jnp.full((8, 128), -4 * cz * nz, jnp.int32)
        for d in range(4 * chunk, min(4 * chunk + 4, nz)):
            for b in range(2):
                box = 2 * column[d] + b
                low = parents[box] * cz + shifts[box] - 1
                target = jnp.where(lane1 // 16 == 2 * (d % 4) + b, low + slot, target)
        target = jnp.where(target == -1, target + nz * cz, target)
        target = jnp.where(target >= nz * cz, target - nz * cz, target)
        target = jnp.where(slot < 10, target - gz * cz, -1)
        for r in range(4):
            sel[chunk, r] = one_hot(roll(target, 32 * r, 1))
    fine_y, fine_z = lane1 // 16, lane1 % 16
    for b in range(2):
        base = (fine_y // 2) * 32 + 16 * b
        expand_t[:, 128 * b : 128 * b + 128] = one_hot(base + fine_z // 2 + 1)
        expand_t[:, 256 + 128 * b : 384 + 128 * b] = one_hot(base + jnp.where(fine_z < 8, 0, 9))
        expand_y[:, 128 * b : 128 * b + 128] = one_hot(16 * b + fine_z // 2 + 1)
    big_lane = lax.broadcasted_iota(jnp.int32, (128, 128), 1)
    for pair in range((nz + 1) // 2):
        target = jnp.full((128, 128), -4 * cz, jnp.int32)
        for k in range(2):
            d = 2 * pair + k
            if d < nz:
                owner = column[(nz - d) % nz]
                for b in range(2):
                    box = 2 * owner + b
                    low = jnp.where(parents[box] == gz, shifts[box], -4 * cz)
                    target = jnp.where(big_row // 32 == 2 * k + b, low, target)
        hit = big_lane == target + big_row % 8
        for y in range(4):
            place[pair, :, 128 * y : 128 * y + 128] = jnp.where(
                hit & ((big_row % 32) // 8 == y), 1.0, 0.0
            )
    count = jnp.zeros((8, 128), F32)
    for box in range(2 * nz):
        low = jnp.where(parents[box] == gz, shifts[box], -4 * cz)
        count = count + jnp.where((lane1 >= low) & (lane1 < low + 8), 1.0, 0.0)
    count = count[0:4]

    ends = take_halos(0, halos)
    rim = [ext[f] for f in range(5)]
    change = coarse_tendency(rim, ends)
    start = to_conserved([a[2:6] for a in rim])
    section = [a + DT_COARSE * b for a, b in zip(start, change)]
    section = to_primitive(section)
    windows = start_windows(0)
    for f in range(5):
        ext[f, 2:6, 2:6, :] = section[f][:, 2:6, :]
    pack_z(section, 1)
    halos = start_halos(1)

    ends = take_halos(1, halos)
    rim = [ext[f] for f in range(5)]
    change = coarse_tendency(rim, ends)
    section = to_conserved([a[2:6] for a in rim])
    for f in range(5):
        new = 0.5 * start[f] + 0.5 * (section[f] + DT_COARSE * change[f])
        upd[f] = new
        ext[f, 2:6, 2:6, :] = new[:, 2:6, :]
        xs1[0, f] = new[:, 2:3, :]
        xs1[1, f] = new[:, 5:6, :]
        ys1[0, f] = new[0, 2:6, :]
        ys1[1, f] = new[3, 2:6, :]
    faces_sent = [
        send(xs1.at[1], xr1.at[0], x_up),
        send(xs1.at[0], xr1.at[1], x_dn),
        send(ys1.at[1], yr1.at[0], y_up),
        send(ys1.at[0], yr1.at[1], y_dn),
    ]

    old_inner, old_faces = take_windows(0, windows)
    cells, ghosts = injected(old_inner, old_faces)
    detail = [fine_density[...]] + [fine_velocity[k] for k in range(3)] + [fine_pressure[...]]
    prim = [a + b for a, b in zip(cells, detail)]
    state = to_conserved(prim)
    rate = fine_tendency(prim, ghosts)
    stage = [a + DT_FINE * b for a, b in zip(state, rate)]

    for copy in faces_sent:
        copy.wait_recv()
    for f in range(5):
        ext[f, 2:6, 1:2, :] = xr1[0, f]
        ext[f, 2:6, 6:7, :] = xr1[1, f]
        ext[f, 1, 2:6, :] = yr1[0, f]
        ext[f, 6, 2:6, :] = yr1[1, f]
    windows = start_windows(1)

    rate = fine_tendency(to_primitive(stage), ghosts)
    state = [0.5 * a + 0.5 * (b + DT_FINE * c) for a, b, c in zip(state, stage, rate)]

    new_inner, new_faces = take_windows(1, windows)

    def middle(old, new):
        mixed = [0.5 * (a + b) for a, b in zip(to_conserved(old), new)]
        mixed[0] = jnp.where(mixed[0] == 0.0, 1.0, mixed[0])
        return to_primitive(mixed)

    _, ghosts = injected(middle(old_inner, new_inner), middle(old_faces, new_faces))
    rate = fine_tendency(to_primitive(state), ghosts)
    stage = [a + DT_FINE * b for a, b in zip(state, rate)]
    rate = fine_tendency(to_primitive(stage), ghosts)
    state = [0.5 * a + 0.5 * (b + DT_FINE * c) for a, b, c in zip(state, stage, rate)]

    child = big_row // 32 * 8 + (big_row % 16) // 2
    flat = []
    for b in range(2):
        flat.append(mm(jnp.concatenate([a[b] for a in state]), jnp.where(big_lane == child + 32 * b, 0.125, 0.0)))
    summed = flat[0] + flat[1]
    summed = summed + roll(summed, -1, 0)
    mean[...] = summed
    mean_got[0] = summed
    copies = [send(mean, mean_got.at[d], {"gz": column[d]}) for d in range(1, nz)]
    for f in range(5):
        fine_out[f] = state[f]
    for copy in copies:
        copy.wait_recv()
    total = None
    for pair in range((nz + 1) // 2):
        both = mean_got[2 * pair]
        if 2 * pair + 1 < nz:
            both = both + roll(mean_got[2 * pair + 1], 64, 1)
        part = mm(both, place[pair])
        total = part if total is None else total + part
    for f in range(5):
        for y in range(4):
            laid[f, y] = total[8 * f : 8 * f + 8, 128 * y : 128 * y + 128]
    for f in range(5):
        for y in range(4):
            value = laid[f, y, pl.ds(0, 4, stride=2), :] / jnp.maximum(count, 1.0)
            coarse_out[f, :, y, :] = jnp.where(count > 0.0, value, upd[f, y, 2:6, :])
    for copy in started:
        copy.wait_send()


def on_device(sizes, density, velocity, pressure, fine_density, fine_velocity, fine_pressure, parent, shift):
    nz = sizes[2]
    fine = fine_density.shape[2:]
    vmem = pl.BlockSpec(memory_space=pltpu.VMEM)
    smem = pl.BlockSpec(memory_space=pltpu.SMEM)
    copies = 16 + 3 * (nz - 1)
    chunks = (nz + 3) // 4
    scratch = [
        (5, 8, 8, 128),
        (2, 2, 5, 4, 2, 128),
        (2, 2, 5, 4, 2, 128),
        (2, 2, 5, 2, 4, 128),
        (2, 2, 5, 2, 4, 128),
        (2, 4, 8, 128),
        (2, 2, 4, 8, 128),
        (2, 5, 4, 1, 128),
        (2, 5, 4, 1, 128),
        (2, 5, 4, 128),
        (2, 5, 4, 128),
        (5, 8, 128),
        (chunks, 4, 128, 128),
        (128, 512),
        (128, 256),
        ((nz + 1) // 2, 128, 512),
        (2, nz - 1, 56, 128),
        (2, nz, 56, 128),
        (40, 128),
        (nz, 40, 128),
        (5, 4, 8, 128),
        (5, 4, 8, 128),
    ]
    coarse, fine_state = pl.pallas_call(
        functools.partial(kernel, sizes),
        out_shape=(
            jax.ShapeDtypeStruct((5,) + density.shape, F32),
            jax.ShapeDtypeStruct((5,) + fine, F32),
        ),
        in_specs=[vmem] * 6 + [smem] * 2,
        out_specs=(vmem, vmem),
        scratch_shapes=[pltpu.VMEM(shape, F32) for shape in scratch]
        + [pltpu.SemaphoreType.DMA((copies,)), pltpu.SemaphoreType.DMA((copies,))],
        compiler_params=pltpu.CompilerParams(
            collective_id=0, has_side_effects=True, vmem_limit_bytes=32 * 1024 * 1024
        ),
    )(
        density,
        velocity,
        pressure,
        fine_density.reshape(fine),
        fine_velocity.reshape((3,) + fine),
        fine_pressure.reshape(fine),
        parent.reshape(-1),
        shift.reshape(-1),
    )
    return coarse, fine_state.reshape((5, 1, 1) + fine)


def solution(mesh):
    sizes = tuple(mesh.shape[axis] for axis in ("gx", "gy", "gz"))
    in_specs = (
        P("gx", "gy", "gz"),
        P(None, "gx", "gy", "gz"),
        P("gx", "gy", "gz"),
        P("gx", "gy", "gz", None, None),
        P(None, "gx", "gy", "gz", None, None),
        P("gx", "gy", "gz", None, None),
        P("gx", "gy", None, None),
        P("gx", "gy", None),
    )
    out_specs = (P(None, "gx", "gy", "gz"), P(None, "gx", "gy", "gz", None, None))
    return jax.shard_map(
        functools.partial(on_device, sizes),
        mesh=mesh,
        in_specs=in_specs,
        out_specs=out_specs,
        check_vma=False,
    )
```

profile of v0, /device:TPU:0, one launch (start us, length us, event | category | flops | bytes accessed | tf_op | source)
XLA Modules:
  0.0 32.4 jit_solution(9815527555514970531)
XLA Ops:
  0.6 0.0 copy-start.2
  0.6 0.0 copy-start.6
  0.7 0.0 copy-start.7
  0.7 0.7 %copy-done.2 = f32[4,4,128]{2,1,0:T(4,128)S(1)} copy-done((f32[4,4,128]{2,1,0:T(4,128)S(1)}, f32[4,4,128]{2,1,0:T(4,128)}, u32[]{:S(2)}) %copy-start.2) | copy-done | bytes 8216
  1.3 0.0 copy-done.6
  1.3 0.0 copy-done.7
  1.3 0.0 copy-start
  1.3 0.7 %copy-done = f32[3,4,4,128]{3,2,1,0:T(4,128)S(1)} copy-done((f32[3,4,4,128]{3,2,1,0:T(4,128)S(1)}, f32[3,4,4,128]{3,2,1,0:T(4,128)}, u32[]{:S(2)}) %copy-start) | copy-done | bytes 24600
  2.1 0.0 copy-start.1
  2.1 0.7 %copy-done.1 = f32[3,1,1,2,8,128]{5,4,3,2,1,0:T(8,128)S(1)} copy-done((f32[3,1,1,2,8,128]{5,4,3,2,1,0:T(8,128)S(1)}, f32[3,1,1,2,8,128]{5,4,3,2,1,0:T(8,128)}, u32[]{:S(2)}) %copy-start.1) | copy-done | bytes 24600
  2.8 0.0 copy-start.3
  2.8 0.7 %copy-done.3 = f32[4,4,128]{2,1,0:T(4,128)S(1)} copy-done((f32[4,4,128]{2,1,0:T(4,128)S(1)}, f32[4,4,128]{2,1,0:T(4,128)}, u32[]{:S(2)}) %copy-start.3) | copy-done | bytes 8216
  3.5 0.0 copy-start.4
  3.5 0.7 %copy-done.4 = f32[1,1,2,8,128]{4,3,2,1,0:T(8,128)S(1)} copy-done((f32[1,1,2,8,128]{4,3,2,1,0:T(8,128)S(1)}, f32[1,1,2,8,128]{4,3,2,1,0:T(8,128)}, u32[]{:S(2)}) %copy-start.4) | copy-done | bytes 8216
  4.2 0.0 copy-start.5
  4.2 0.7 %copy-done.5 = f32[1,1,2,8,128]{4,3,2,1,0:T(8,128)S(1)} copy-done((f32[1,1,2,8,128]{4,3,2,1,0:T(8,128)S(1)}, f32[1,1,2,8,128]{4,3,2,1,0:T(8,128)}, u32[]{:S(2)}) %copy-start.5) | copy-done | bytes 8216
  4.9 26.2 %shard_map.95 = (f32[5,4,4,128]{3,2,1,0:T(4,128)S(1)}, f32[5,2,8,128]{3,2,1,0:T(8,128)S(1)}) custom-call(f32[4,4,128]{2,1,0:T(4,128)S(1)} %copy-done.2, f32[3,4,4,128]{3,2,1,0:T(4,128)S(1)} %copy-done, f32[4,4,128]{2,1,0:T(4,128)S(1)} %copy-done.3, f32[2,8,128]{2,1,0:T(8,128)S(1)} %bitcast.10, f32[3,2,8,128]{3,2,1,0:T(8,128)S(1)} %bitcast.9, ...), custom_call_target="tpu_custom_call" | custom-call | tf_op jit(solution)/shard_map/pallas_call | solution.py:527
  31.1 0.6 %copy.13 = f32[5,4,4,128]{3,2,1,0:T(4,128)} copy(f32[5,4,4,128]{3,2,1,0:T(4,128)S(1)} %get-tuple-element.10) | data formatting | bytes 81920
  31.8 0.6 %copy.14 = f32[5,1,1,2,8,128]{5,4,3,2,1,0:T(8,128)} copy(f32[5,1,1,2,8,128]{5,4,3,2,1,0:T(8,128)S(1)} %bitcast.8) | data formatting | bytes 81920
Async XLA Ops:
  0.6 0.7 %copy-start.2 = (f32[4,4,128]{2,1,0:T(4,128)S(1)}, f32[4,4,128]{2,1,0:T(4,128)}, u32[]{:S(2)}) copy-start(f32[4,4,128]{2,1,0:T(4,128)} %density.1) | copy-start | bytes 24580
  0.6 0.7 %copy-start.6 = (s32[1,1,8,1]{2,3,1,0:T(1,128)S(1)}, s32[1,1,8,1]{2,3,1,0:T(1,128)}, u32[]{:S(2)}) copy-start(s32[1,1,8,1]{2,3,1,0:T(1,128)} %param.14) | copy-start | bytes 100
  0.7 0.7 %copy-start.7 = (s32[1,1,8]{2,1,0:T(1,128)S(1)}, s32[1,1,8]{2,1,0:T(1,128)}, u32[]{:S(2)}) copy-start(s32[1,1,8]{2,1,0:T(1,128)} %param.15) | copy-start | bytes 100
  1.3 0.7 %copy-start = (f32[3,4,4,128]{3,2,1,0:T(4,128)S(1)}, f32[3,4,4,128]{3,2,1,0:T(4,128)}, u32[]{:S(2)}) copy-start(f32[3,4,4,128]{3,2,1,0:T(4,128)} %velocity.1) | copy-start | bytes 73732
  2.1 0.7 %copy-start.1 = (f32[3,1,1,2,8,128]{5,4,3,2,1,0:T(8,128)S(1)}, f32[3,1,1,2,8,128]{5,4,3,2,1,0:T(8,128)}, u32[]{:S(2)}) copy-start(f32[3,1,1,2,8,128]{5,4,3,2,1,0:T(8,128)} %param.12) | copy-start | bytes 73732
  2.8 0.7 %copy-start.3 = (f32[4,4,128]{2,1,0:T(4,128)S(1)}, f32[4,4,128]{2,1,0:T(4,128)}, u32[]{:S(2)}) copy-start(f32[4,4,128]{2,1,0:T(4,128)} %pressure.1) | copy-start | bytes 24580
  3.5 0.7 %copy-start.4 = (f32[1,1,2,8,128]{4,3,2,1,0:T(8,128)S(1)}, f32[1,1,2,8,128]{4,3,2,1,0:T(8,128)}, u32[]{:S(2)}) copy-start(f32[1,1,2,8,128]{4,3,2,1,0:T(8,128)} %param.11) | copy-start | bytes 24580
  4.2 0.7 %copy-start.5 = (f32[1,1,2,8,128]{4,3,2,1,0:T(8,128)S(1)}, f32[1,1,2,8,128]{4,3,2,1,0:T(8,128)}, u32[]{:S(2)}) copy-start(f32[1,1,2,8,128]{4,3,2,1,0:T(8,128)} %param.13) | copy-start | bytes 24580
where the time goes:
time: 32.8 us; the launch traced here: 32.4 us
  Pallas kernels  26.2 us (80%)
  local copies, waits for them, and re-layouts  5.48 us (17%)
  between operations  0.67 us (2%)
    pallas_call x1, Pallas kernels, on_device(): pl.pallas_call(functools.partial(kernel, sizes), out_shape=(jax.ShapeDtyp...  26.2 us
    unnamed x18, local copies, waits for them, and re-layouts  5.48 us

commit v1 on v0

--- a/solution.py
+++ b/solution.py
@@ -12,16 +12,17 @@
 DT_FINE = 0.025
 MESH = pl.DeviceIdType.MESH
 F32 = jnp.float32
+BF16 = jnp.bfloat16
 
 
 def mm(a, b):
-    return lax.dot_general(
-        a,
-        b,
-        (((1,), (0,)), ((), ())),
-        precision=lax.Precision.HIGHEST,
-        preferred_element_type=F32,
-    )
+    size = a.shape[0]
+    high = a.astype(BF16).astype(F32)
+    rest = a - high
+    middle = rest.astype(BF16).astype(F32)
+    parts = jnp.concatenate([high, middle, rest - middle]).astype(BF16)
+    out = lax.dot_general(parts, b, (((1,), (0,)), ((), ())), preferred_element_type=F32)
+    return (out[0:size] + out[size : 2 * size]) + out[2 * size : 3 * size]
 
 
 def to_conserved(q):
@@ -172,16 +173,24 @@
 
 def kernel(
     sizes,
+    density_in,
+    velocity_in,
+    pressure_in,
+    fine_density_in,
+    fine_velocity_in,
+    fine_pressure_in,
+    parents_in,
+    shifts_in,
+    coarse_to,
+    fine_to,
+    coarse_out,
+    fine_out,
     density,
     velocity,
     pressure,
     fine_density,
     fine_velocity,
     fine_pressure,
-    parents,
-    shifts,
-    coarse_out,
-    fine_out,
     ext,
     xs,
     xr,
@@ -194,16 +203,19 @@
     ys1,
     yr1,
     yf,
-    sel,
-    expand_t,
-    expand_y,
-    place,
     msg,
     got,
     mean,
     mean_got,
     laid,
     upd,
+    sel,
+    expand_t,
+    expand_y,
+    place,
+    parents,
+    shifts,
+    load_sem,
     send_sem,
     recv_sem,
 ):
@@ -230,6 +242,21 @@
         started.append(copy)
         return copy
 
+    loads = []
+    for src, dst in (
+        (density_in, density),
+        (velocity_in, velocity),
+        (pressure_in, pressure),
+        (parents_in, parents),
+        (shifts_in, shifts),
+        (fine_density_in, fine_density),
+        (fine_velocity_in, fine_velocity),
+        (fine_pressure_in, fine_pressure),
+    ):
+        load = pltpu.make_async_copy(src, dst, load_sem.at[len(loads)])
+        load.start()
+        loads.append(load)
+
     barrier = pltpu.get_barrier_semaphore()
     partners = [x_up, x_dn, y_up, y_dn] + [{"gz": column[d]} for d in range(1, nz)]
     for device in partners:
@@ -244,12 +271,13 @@
             packed = jnp.where(lane3 // 4 == f, roll(fields[f], 2 + 4 * f, 2), packed)
         zs[at] = packed
 
-    def start_halos(at):
+    def start_halos(fields, at):
+        pack_z(fields, at)
         for f in range(5):
-            xs[at, 0, f] = ext[f, 2:6, 2:4, :]
-            xs[at, 1, f] = ext[f, 2:6, 4:6, :]
-            ys[at, 0, f] = ext[f, 2:4, 2:6, :]
-            ys[at, 1, f] = ext[f, 4:6, 2:6, :]
+            xs[at, 0, f] = fields[f][:, 2:4, :]
+            xs[at, 1, f] = fields[f][:, 4:6, :]
+            ys[at, 0, f] = fields[f][0:2, 2:6, :]
+            ys[at, 1, f] = fields[f][2:4, 2:6, :]
         if at == 0:
             pl.semaphore_wait(barrier, len(partners))
         return [
@@ -282,7 +310,7 @@
             for r in range(4):
                 rows = [ext[f, 2 + r] for f in range(5)] + [yf[r]]
                 if r == 0:
-                    rows.append(yf[4])
+                    rows += [yf[4], yf[4]]
                 picked.append(mm(jnp.concatenate(rows), sel[chunk, r]))
             for d in range(4 * chunk, min(4 * chunk + 4, nz)):
                 body = jnp.zeros((48, 128), F32)
@@ -344,18 +372,21 @@
         return cells, (in_x, in_y, in_z)
 
     ext[...] = jnp.ones(ext.shape, F32)
+    for load in loads[0:3]:
+        load.wait()
     for y in range(4):
         ext[0, 2 + y, 2:6, :] = density[:, y, :]
         for k in range(3):
             ext[1 + k, 2 + y, 2:6, :] = velocity[k, :, y, :]
         ext[4, 2 + y, 2:6, :] = pressure[:, y, :]
-    pack_z([ext[f, 2:6] for f in range(5)], 0)
-    halos = start_halos(0)
+    halos = start_halos([ext[f, 2:6] for f in range(5)], 0)
+    for load in loads[3:8]:
+        load.wait()
 
     big_row = lax.broadcasted_iota(jnp.int32, (128, 128), 0)
 
     def one_hot(index):
-        return jnp.where(big_row == index[0:1, :], 1.0, 0.0)
+        return jnp.where(big_row == index[0:1, :], 1.0, 0.0).astype(BF16)
 
     slot = lane1 % 16
     for chunk in range((nz + 3) // 4):
@@ -389,14 +420,15 @@
                     target = jnp.where(big_row // 32 == 2 * k + b, low, target)
         hit = big_lane == target + big_row % 8
         for y in range(4):
-            place[pair, :, 128 * y : 128 * y + 128] = jnp.where(
+            place[128 * pair : 128 * pair + 128, 128 * y : 128 * y + 128] = jnp.where(
                 hit & ((big_row % 32) // 8 == y), 1.0, 0.0
-            )
+            ).astype(BF16)
     count = jnp.zeros((8, 128), F32)
     for box in range(2 * nz):
         low = jnp.where(parents[box] == gz, shifts[box], -4 * cz)
         count = count + jnp.where((lane1 >= low) & (lane1 < low + 8), 1.0, 0.0)
-    count = count[0:4]
+    covered = count[0:4] > 0.0
+    share = 1.0 / jnp.maximum(count[0:4], 1.0)
 
     ends = take_halos(0, halos)
     rim = [ext[f] for f in range(5)]
@@ -404,11 +436,10 @@
     start = to_conserved([a[2:6] for a in rim])
     section = [a + DT_COARSE * b for a, b in zip(start, change)]
     section = to_primitive(section)
+    halos = start_halos(section, 1)
     windows = start_windows(0)
     for f in range(5):
         ext[f, 2:6, 2:6, :] = section[f][:, 2:6, :]
-    pack_z(section, 1)
-    halos = start_halos(1)
 
     ends = take_halos(1, halos)
     rim = [ext[f] for f in range(5)]
@@ -463,44 +494,65 @@
     state = [0.5 * a + 0.5 * (b + DT_FINE * c) for a, b, c in zip(state, stage, rate)]
 
     child = big_row // 32 * 8 + (big_row % 16) // 2
-    flat = []
-    for b in range(2):
-        flat.append(mm(jnp.concatenate([a[b] for a in state]), jnp.where(big_lane == child + 32 * b, 0.125, 0.0)))
-    summed = flat[0] + flat[1]
+    matrix = jnp.where(big_lane == child, 0.125, 0.0).astype(BF16)
+    flat = mm(jnp.concatenate([a[b] for b in range(2) for a in state]), matrix)
+    summed = flat[0:40] + roll(flat[40:80], 32, 1)
     summed = summed + roll(summed, -1, 0)
     mean[...] = summed
     mean_got[0] = summed
     copies = [send(mean, mean_got.at[d], {"gz": column[d]}) for d in range(1, nz)]
     for f in range(5):
         fine_out[f] = state[f]
+    fine_store = pltpu.make_async_copy(fine_out, fine_to, load_sem.at[8])
+    fine_store.start()
     for copy in copies:
         copy.wait_recv()
-    total = None
+    rows = []
     for pair in range((nz + 1) // 2):
         both = mean_got[2 * pair]
         if 2 * pair + 1 < nz:
             both = both + roll(mean_got[2 * pair + 1], 64, 1)
-        part = mm(both, place[pair])
-        total = part if total is None else total + part
+        rows.append(jnp.concatenate([both, jnp.zeros((8, 128), F32)]))
+    total = mm(jnp.concatenate(rows, axis=1), place[...])
     for f in range(5):
         for y in range(4):
             laid[f, y] = total[8 * f : 8 * f + 8, 128 * y : 128 * y + 128]
     for f in range(5):
         for y in range(4):
-            value = laid[f, y, pl.ds(0, 4, stride=2), :] / jnp.maximum(count, 1.0)
-            coarse_out[f, :, y, :] = jnp.where(count > 0.0, value, upd[f, y, 2:6, :])
+            value = laid[f, y, pl.ds(0, 4, stride=2), :] * share
+            coarse_out[f, :, y, :] = jnp.where(covered, value, upd[f, y, 2:6, :])
+    coarse_store = pltpu.make_async_copy(coarse_out, coarse_to, load_sem.at[9])
+    coarse_store.start()
     for copy in started:
         copy.wait_send()
+    fine_store.wait()
+    coarse_store.wait()
+
+
+def hand_over(coarse, fine, coarse_out, fine_out, sems):
+    first = pltpu.make_async_copy(coarse, coarse_out, sems.at[0])
+    second = pltpu.make_async_copy(fine, fine_out, sems.at[1])
+    first.start()
+    second.start()
+    first.wait()
+    second.wait()
 
 
 def on_device(sizes, density, velocity, pressure, fine_density, fine_velocity, fine_pressure, parent, shift):
     nz = sizes[2]
     fine = fine_density.shape[2:]
-    vmem = pl.BlockSpec(memory_space=pltpu.VMEM)
-    smem = pl.BlockSpec(memory_space=pltpu.SMEM)
+    hbm = pl.BlockSpec(memory_space=pltpu.HBM)
     copies = 16 + 3 * (nz - 1)
     chunks = (nz + 3) // 4
     scratch = [
+        (5,) + density.shape,
+        (5,) + fine,
+        density.shape,
+        velocity.shape,
+        pressure.shape,
+        fine,
+        (3,) + fine,
+        fine,
         (5, 8, 8, 128),
         (2, 2, 5, 4, 2, 128),
         (2, 2, 5, 4, 2, 128),
@@ -513,10 +565,6 @@
         (2, 5, 4, 128),
         (2, 5, 4, 128),
         (5, 8, 128),
-        (chunks, 4, 128, 128),
-        (128, 512),
-        (128, 256),
-        ((nz + 1) // 2, 128, 512),
         (2, nz - 1, 56, 128),
         (2, nz, 56, 128),
         (40, 128),
@@ -524,18 +572,21 @@
         (5, 4, 8, 128),
         (5, 4, 8, 128),
     ]
+    matrices = [(chunks, 4, 128, 128), (128, 512), (128, 256), (128 * ((nz + 1) // 2), 512)]
     coarse, fine_state = pl.pallas_call(
         functools.partial(kernel, sizes),
         out_shape=(
             jax.ShapeDtypeStruct((5,) + density.shape, F32),
             jax.ShapeDtypeStruct((5,) + fine, F32),
         ),
-        in_specs=[vmem] * 6 + [smem] * 2,
-        out_specs=(vmem, vmem),
+        in_specs=[hbm] * 8,
+        out_specs=(hbm, hbm),
         scratch_shapes=[pltpu.VMEM(shape, F32) for shape in scratch]
-        + [pltpu.SemaphoreType.DMA((copies,)), pltpu.SemaphoreType.DMA((copies,))],
+        + [pltpu.VMEM(shape, BF16) for shape in matrices]
+        + [pltpu.SMEM((2 * nz,), jnp.int32)] * 2
+        + [pltpu.SemaphoreType.DMA((10,)), pltpu.SemaphoreType.DMA((copies,)), pltpu.SemaphoreType.DMA((copies,))],
         compiler_params=pltpu.CompilerParams(
-            collective_id=0, has_side_effects=True, vmem_limit_bytes=32 * 1024 * 1024
+            collective_id=0, has_side_effects=True, vmem_limit_bytes=56 * 1024 * 1024
         ),
     )(
         density,
@@ -547,6 +598,17 @@
         parent.reshape(-1),
         shift.reshape(-1),
     )
+    coarse, fine_state = pl.pallas_call(
+        hand_over,
+        out_shape=(
+            jax.ShapeDtypeStruct(coarse.shape, F32),
+            jax.ShapeDtypeStruct(fine_state.shape, F32),
+        ),
+        in_specs=[hbm, hbm],
+        out_specs=(hbm, hbm),
+        scratch_shapes=[pltpu.SemaphoreType.DMA((2,))],
+        compiler_params=pltpu.CompilerParams(vmem_limit_bytes=56 * 1024 * 1024),
+    )(coarse, fine_state)
     return coarse, fine_state.reshape((5, 1, 1) + fine)
 
 

time: 32.8 us -> 30 us (0.915)
  local copies, waits for them, and re-layouts: 5.48 us -> 0 us
  Pallas kernels: 26.2 us -> 29.2 us
    unnamed x18 -> x0, local copies, waits for them, and re-layouts: 5.48 us -> none
    pallas_call x0 -> x1, Pallas kernels: none -> 3.6 us  [on_device(): pl.pallas_call(hand_over, out_shape=(jax.ShapeDtypeStruct(coarse.shape, F...]
    pallas_call x1, Pallas kernels: 26.2 us -> 25.6 us  [on_device(): pl.pallas_call(functools.partial(kernel, sizes), out_shape=(jax.ShapeDtyp...]
where the time goes in v1:
time: 30 us; the launch traced here: 29.8 us
  Pallas kernels  29.2 us (97%)
  between operations  0.64 us (2%)
    pallas_call x1, Pallas kernels, on_device(): pl.pallas_call(functools.partial(kernel, sizes), out_shape=(jax.ShapeDtyp...  25.6 us
    pallas_call x1, Pallas kernels, on_device(): pl.pallas_call(hand_over, out_shape=(jax.ShapeDtypeStruct(coarse.shape, F...  3.6 us

profile of v1, /device:TPU:0, one launch (start us, length us, event | category | flops | bytes accessed | tf_op | source)
XLA Modules:
  0.0 29.8 jit_solution(2674383326264022200)
XLA Ops:
  0.6 25.6 %shard_map.95 = (f32[5,4,4,128]{3,2,1,0:T(4,128)}, f32[5,2,8,128]{3,2,1,0:T(8,128)}) custom-call(f32[4,4,128]{2,1,0:T(4,128)} %density_in.1, f32[3,4,4,128]{3,2,1,0:T(4,128)} %velocity_in.1, f32[4,4,128]{2,1,0:T(4,128)} %pressure_in.1, f32[2,8,128]{2,1,0:T(8,128)} %bitcast.9, f32[3,2,8,128]{3,2,1,0:T(8,128)} %bitcast.8, f32[2,8,128]{2,1,0:T(8,128)} %bitcast.10, ...), custom_call_target="tpu_custom_call" | custom-call | tf_op jit(solution)/shard_map/pallas_call | solution.py:576
  26.2 3.6 %shard_map.96 = (f32[5,4,4,128]{3,2,1,0:T(4,128)}, f32[5,2,8,128]{3,2,1,0:T(8,128)}) custom-call(f32[5,4,4,128]{3,2,1,0:T(4,128)} %get-tuple-element.6.coarse, f32[5,2,8,128]{3,2,1,0:T(8,128)} %get-tuple-element.7.fine), custom_call_target="tpu_custom_call" | custom-call | tf_op jit(solution)/shard_map/pallas_call | solution.py:601

commit v2 on v1

--- a/solution.py
+++ b/solution.py
@@ -97,11 +97,11 @@
     return a if shift == 0 else pltpu.roll(a, shift, axis)
 
 
-def coarse_tendency(q, n):
+def coarse_fluxes_yz(q, n):
     lane = lax.broadcasted_iota(jnp.int32, (1, 8, 128), 2)
     row = lax.broadcasted_iota(jnp.int32, (1, 8, 128), 1)
     inner = (row >= 2) & (row < 6)
-    ly, ry, lx, rx, lz, rz = [], [], [], [], [], []
+    ly, ry, lz, rz = [], [], [], []
     for f in range(5):
         a = q[f]
         jump = a[1:8] - a[0:7]
@@ -109,10 +109,6 @@
         ly.append(a[1:6] + half[0:5])
         ry.append(a[2:7] - half[1:6])
         c = a[2:6]
-        jump = c - roll(c, 1, 1)
-        half = 0.5 * minmod(jump, roll(jump, -1, 1))
-        lx.append(roll(c + half, 1, 1))
-        rx.append(c - half)
         g = n[f]
         before = roll(jnp.where(lane == 127, g, c), 1, 2)
         after = roll(jnp.where(lane == 0, g, c), -1, 2)
@@ -126,14 +122,24 @@
         high_right = roll(jnp.where(lane == 0, g - g_half, down), -1, 2)
         lz.append(jnp.where(inner, low_left, roll(up, 4, 1)))
         rz.append(jnp.where(inner, down, roll(high_right, 4, 1)))
-    fx, fy, fz = stacked_flux([(0, lx), (1, ly), (2, lz)], [(0, rx), (1, ry), (2, rz)])
+    fy, fz = stacked_flux([(1, ly), (2, lz)], [(1, ry), (2, rz)])
     out = []
     for f in range(5):
-        dx = roll(fx[f], -1, 1) - fx[f]
         dy = fy[f][1:5] - fy[f][0:4]
         dz = roll(fz[f], 4, 1) - fz[f]
-        out.append(-dx - dy - dz)
+        out.append(-dy - dz)
     return out
+
+
+def coarse_fluxes_x(q):
+    lx, rx = [], []
+    for c in q:
+        jump = c - roll(c, 1, 1)
+        half = 0.5 * minmod(jump, roll(jump, -1, 1))
+        lx.append(roll(c + half, 1, 1))
+        rx.append(c - half)
+    (fx,) = stacked_flux([(0, lx)], [(0, rx)])
+    return [a - roll(a, -1, 1) for a in fx]
 
 
 def fine_tendency(q, ghosts):
@@ -142,6 +148,13 @@
     firsts = (row == 0, lane < 16, lane % 16 == 0)
     lasts = (row == 7, lane >= 112, lane % 16 == 15)
     steps = ((1, 1), (16, 2), (1, 2))
+    moves = ((4, 1), (64, 2), (8, 2))
+    halves = (row >= 4, lane >= 64, lane % 16 >= 8)
+
+    def shared(fields, axis):
+        move, dim = moves[axis]
+        return [jnp.where(halves[axis], a[0:1], roll(a[1:2], move, dim)) for a in fields]
+
     lefts, rights, end_lefts, end_rights = [], [], [], []
     for axis in range(3):
         step, dim = steps[axis]
@@ -158,15 +171,17 @@
             tops.append(up)
         lefts.append((axis, left))
         rights.append((axis, right))
-        end_lefts.append((axis, tops))
-        end_rights.append((axis, ghosts[axis]))
+        end_lefts.append((axis, shared(tops, axis)))
+        end_rights.append((axis, shared(ghosts[axis], axis)))
     parts = stacked_flux(lefts + end_lefts, rights + end_rights)
     out = [None] * 5
     for axis in range(3):
         step, dim = steps[axis]
         for f in range(5):
             low = parts[axis][f]
-            change = jnp.where(lasts[axis], parts[3 + axis][f], roll(low, -step, dim)) - low
+            top = parts[3 + axis][f]
+            top = jnp.concatenate([top, roll(top, -moves[axis][0], dim)])
+            change = jnp.where(lasts[axis], top, roll(low, -step, dim)) - low
             out[f] = -change if out[f] is None else out[f] - change
     return [2.0 * part for part in out]
 
@@ -181,8 +196,6 @@
     fine_pressure_in,
     parents_in,
     shifts_in,
-    coarse_to,
-    fine_to,
     coarse_out,
     fine_out,
     density,
@@ -203,8 +216,13 @@
     ys1,
     yr1,
     yf,
+    xf,
     msg,
     got,
+    msg_z,
+    got_z,
+    msg_f,
+    got_f,
     mean,
     mean_got,
     laid,
@@ -289,53 +307,61 @@
             send(zs.at[at], zr.at[at, 1], z_dn),
         ]
 
-    def take_halos(at, copies):
-        for copy in copies:
+    def coarse_stage(at, copies):
+        for copy in copies[2:6]:
+            copy.wait_recv()
+        for f in range(5):
+            ext[f, 0:2, 2:6, :] = yr[at, 0, f]
+            ext[f, 6:8, 2:6, :] = yr[at, 1, f]
+        ends = jnp.where(lane3 % 4 < 2, zr[at, 0], zr[at, 1])
+        ends = [roll(ends, 126 - 4 * f, 2) for f in range(5)]
+        change = coarse_fluxes_yz([ext[f] for f in range(5)], ends)
+        for copy in copies[0:2]:
             copy.wait_recv()
         for f in range(5):
             ext[f, 2:6, 0:2, :] = xr[at, 0, f]
             ext[f, 2:6, 6:8, :] = xr[at, 1, f]
-            ext[f, 0:2, 2:6, :] = yr[at, 0, f]
-            ext[f, 6:8, 2:6, :] = yr[at, 1, f]
-        ends = jnp.where(lane3 % 4 < 2, zr[at, 0], zr[at, 1])
-        return [roll(ends, 126 - 4 * f, 2) for f in range(5)]
-
-    def start_windows(at):
-        for f in range(5):
-            yf[f, 0:4, :] = ext[f, 1, 2:6, :]
-            yf[f, 4:8, :] = ext[f, 6, 2:6, :]
+        block = [ext[f, 2:6] for f in range(5)]
+        change = [a + b for a, b in zip(change, coarse_fluxes_x(block))]
+        return block, change
+
+    group = lax.broadcasted_iota(jnp.int32, (48, 128), 1) // 32
+
+    def start_picked(rows, size, out, into):
         copies = []
         for chunk in range((nz + 3) // 4):
-            picked = []
-            for r in range(4):
-                rows = [ext[f, 2 + r] for f in range(5)] + [yf[r]]
-                if r == 0:
-                    rows += [yf[4], yf[4]]
-                picked.append(mm(jnp.concatenate(rows), sel[chunk, r]))
+            picked = [mm(rows[r], sel[chunk, r]) for r in range(4)]
             for d in range(4 * chunk, min(4 * chunk + 4, nz)):
-                body = jnp.zeros((48, 128), F32)
-                group = lax.broadcasted_iota(jnp.int32, (48, 128), 1) // 32
+                body = jnp.zeros((size, 128), F32)
                 for r in range(4):
-                    body = jnp.where(group == (d + r) % 4, picked[r][0:48], body)
-                tail = jnp.where(lane1 // 32 == d % 4, picked[0][48:56], 0.0)
-                if d == 0:
-                    got[at, 0, 0:48, :] = body
-                    got[at, 0, 48:56, :] = tail
-                else:
-                    msg[at, d - 1, 0:48, :] = body
-                    msg[at, d - 1, 48:56, :] = tail
-                    copies.append(send(msg.at[at, d - 1], got.at[at, d], {"gz": column[d]}))
+                    body = jnp.where(group[0:size] == (d + r) % 4, picked[r][0:size], body)
+                parts = [(0, size, body)]
+                total = into.shape[1]
+                if total > size:
+                    tail = jnp.where(lane1 // 32 == d % 4, picked[0][size:total], 0.0)
+                    parts.append((size, total, tail))
+                for low, high, part in parts:
+                    if d == 0:
+                        into[0, low:high, :] = part
+                    else:
+                        out[d - 1, low:high, :] = part
+                if d > 0:
+                    copies.append(send(out.at[d - 1], into.at[d], {"gz": column[d]}))
         return copies
 
-    def take_windows(at, copies):
+    def take_picked(copies, into):
         for copy in copies:
             copy.wait_recv()
-        total = got[at, 0]
+        total = into[0]
         for d in range(1, nz):
-            total = total + roll(got[at, d], -32 * (d % 4), 1)
-        inner = [total[8 * f : 8 * f + 8] for f in range(5)]
-        faces = [roll(total[40:48], -32 * f, 1) for f in range(4)] + [total[48:56]]
-        return inner, faces
+            total = total + roll(into[d], -32 * (d % 4), 1)
+        return total
+
+    def tiles(total, count):
+        return [total[8 * k : 8 * k + 8] for k in range(count)]
+
+    def turned(first, last):
+        return [roll(first, -32 * f, 1) for f in range(4)] + [last]
 
     row2 = lax.broadcasted_iota(jnp.int32, (8, 128), 0)
 
@@ -430,25 +456,26 @@
     covered = count[0:4] > 0.0
     share = 1.0 / jnp.maximum(count[0:4], 1.0)
 
-    ends = take_halos(0, halos)
-    rim = [ext[f] for f in range(5)]
-    change = coarse_tendency(rim, ends)
-    start = to_conserved([a[2:6] for a in rim])
+    block, change = coarse_stage(0, halos)
+    start = to_conserved(block)
     section = [a + DT_COARSE * b for a, b in zip(start, change)]
     section = to_primitive(section)
     halos = start_halos(section, 1)
-    windows = start_windows(0)
+    for f in range(5):
+        yf[f, 0:4, :] = ext[f, 1, 2:6, :]
+        yf[f, 4:8, :] = ext[f, 6, 2:6, :]
+    rows = []
+    for r in range(4):
+        rows.append(jnp.concatenate([ext[f, 2 + r] for f in range(5)] + [yf[r], yf[4], yf[4]]))
+    windows = start_picked(rows, 48, msg, got)
     for f in range(5):
         ext[f, 2:6, 2:6, :] = section[f][:, 2:6, :]
 
-    ends = take_halos(1, halos)
-    rim = [ext[f] for f in range(5)]
-    change = coarse_tendency(rim, ends)
-    section = to_conserved([a[2:6] for a in rim])
+    block, change = coarse_stage(1, halos)
+    section = to_conserved(block)
     for f in range(5):
         new = 0.5 * start[f] + 0.5 * (section[f] + DT_COARSE * change[f])
         upd[f] = new
-        ext[f, 2:6, 2:6, :] = new[:, 2:6, :]
         xs1[0, f] = new[:, 2:3, :]
         xs1[1, f] = new[:, 5:6, :]
         ys1[0, f] = new[0, 2:6, :]
@@ -460,7 +487,13 @@
         send(ys1.at[0], yr1.at[1], y_dn),
     ]
 
-    old_inner, old_faces = take_windows(0, windows)
+    rows = []
+    for r in range(4):
+        rows.append(jnp.concatenate([upd[f, r] for f in range(5)] + [upd[4, r]]))
+    near = start_picked(rows, 40, msg_z, got_z)
+
+    total = take_picked(windows, got)
+    old_inner, old_faces = tiles(total, 5), turned(total[40:48], total[48:56])
     cells, ghosts = injected(old_inner, old_faces)
     detail = [fine_density[...]] + [fine_velocity[k] for k in range(3)] + [fine_pressure[...]]
     prim = [a + b for a, b in zip(cells, detail)]
@@ -470,17 +503,24 @@
 
     for copy in faces_sent:
         copy.wait_recv()
-    for f in range(5):
-        ext[f, 2:6, 1:2, :] = xr1[0, f]
-        ext[f, 2:6, 6:7, :] = xr1[1, f]
-        ext[f, 1, 2:6, :] = yr1[0, f]
-        ext[f, 6, 2:6, :] = yr1[1, f]
-    windows = start_windows(1)
+    xf[...] = jnp.zeros(xf.shape, F32)
+    for f in range(5):
+        xf[:, f, :] = xr1[0, f, :, 0, :]
+        xf[:, 8 + f, :] = xr1[1, f, :, 0, :]
+        yf[f, 0:4, :] = yr1[0, f]
+        yf[f, 4:8, :] = yr1[1, f]
+    rows = [jnp.concatenate([xf[r], yf[r], yf[4]]) for r in range(4)]
+    far = start_picked(rows, 24, msg_f, got_f)
 
     rate = fine_tendency(to_primitive(stage), ghosts)
     state = [0.5 * a + 0.5 * (b + DT_FINE * c) for a, b, c in zip(state, stage, rate)]
 
-    new_inner, new_faces = take_windows(1, windows)
+    new_inner = tiles(take_picked(near, got_z), 5)
+    total = take_picked(far, got_f)
+    for f in range(5):
+        side = jnp.where(row2 == 1, total[f : f + 1], total[8 + f : 9 + f])
+        new_inner[f] = jnp.where((row2 >= 2) & (row2 < 6), new_inner[f], side)
+    new_faces = turned(total[16:24], total[24:32])
 
     def middle(old, new):
         mixed = [0.5 * (a + b) for a, b in zip(to_conserved(old), new)]
@@ -498,35 +538,36 @@
     flat = mm(jnp.concatenate([a[b] for b in range(2) for a in state]), matrix)
     summed = flat[0:40] + roll(flat[40:80], 32, 1)
     summed = summed + roll(summed, -1, 0)
-    mean[...] = summed
-    mean_got[0] = summed
+    keep = (row2 % 2 == 0) & (lane1 < 64)
+    parts = [jnp.where(keep, tile, 0.0) for tile in tiles(summed, 5)]
+    odd = roll(parts[2] + roll(parts[3], 64, 1), 1, 0)
+    packed = jnp.concatenate([parts[0] + roll(parts[1], 64, 1) + odd, parts[4]])
+    mean[...] = packed
+    mean_got[0] = packed
     copies = [send(mean, mean_got.at[d], {"gz": column[d]}) for d in range(1, nz)]
     for f in range(5):
         fine_out[f] = state[f]
-    fine_store = pltpu.make_async_copy(fine_out, fine_to, load_sem.at[8])
-    fine_store.start()
     for copy in copies:
         copy.wait_recv()
     rows = []
     for pair in range((nz + 1) // 2):
-        both = mean_got[2 * pair]
-        if 2 * pair + 1 < nz:
-            both = both + roll(mean_got[2 * pair + 1], 64, 1)
-        rows.append(jnp.concatenate([both, jnp.zeros((8, 128), F32)]))
+        here = mean_got[2 * pair]
+        there = mean_got[2 * pair + 1] if 2 * pair + 1 < nz else jnp.zeros((16, 128), F32)
+        first = jnp.where(lane1 < 64, here[0:8], roll(there[0:8], 64, 1))
+        second = jnp.where(lane1 < 64, roll(here[0:8], 64, 1), there[0:8])
+        third = jnp.where(lane1 < 64, here[8:16], roll(there[8:16], 64, 1))
+        rows.append(jnp.concatenate([first, second, third, third]))
     total = mm(jnp.concatenate(rows, axis=1), place[...])
-    for f in range(5):
+    for k in range(3):
         for y in range(4):
-            laid[f, y] = total[8 * f : 8 * f + 8, 128 * y : 128 * y + 128]
-    for f in range(5):
+            laid[k, y] = total[8 * k : 8 * k + 8, 128 * y : 128 * y + 128]
+    for f in range(5):
+        tile, at = ((0, 0), (1, 0), (0, 1), (1, 1), (2, 0))[f]
         for y in range(4):
-            value = laid[f, y, pl.ds(0, 4, stride=2), :] * share
+            value = laid[tile, y, pl.ds(at, 4, stride=2), :] * share
             coarse_out[f, :, y, :] = jnp.where(covered, value, upd[f, y, 2:6, :])
-    coarse_store = pltpu.make_async_copy(coarse_out, coarse_to, load_sem.at[9])
-    coarse_store.start()
     for copy in started:
         copy.wait_send()
-    fine_store.wait()
-    coarse_store.wait()
 
 
 def hand_over(coarse, fine, coarse_out, fine_out, sems):
@@ -541,12 +582,11 @@
 def on_device(sizes, density, velocity, pressure, fine_density, fine_velocity, fine_pressure, parent, shift):
     nz = sizes[2]
     fine = fine_density.shape[2:]
+    vmem = pl.BlockSpec(memory_space=pltpu.VMEM)
     hbm = pl.BlockSpec(memory_space=pltpu.HBM)
-    copies = 16 + 3 * (nz - 1)
+    copies = 16 + 4 * (nz - 1)
     chunks = (nz + 3) // 4
     scratch = [
-        (5,) + density.shape,
-        (5,) + fine,
         density.shape,
         velocity.shape,
         pressure.shape,
@@ -565,26 +605,31 @@
         (2, 5, 4, 128),
         (2, 5, 4, 128),
         (5, 8, 128),
-        (2, nz - 1, 56, 128),
-        (2, nz, 56, 128),
-        (40, 128),
+        (4, 16, 128),
+        (nz - 1, 56, 128),
+        (nz, 56, 128),
+        (nz - 1, 40, 128),
         (nz, 40, 128),
-        (5, 4, 8, 128),
+        (nz - 1, 32, 128),
+        (nz, 32, 128),
+        (16, 128),
+        (nz, 16, 128),
+        (3, 4, 8, 128),
         (5, 4, 8, 128),
     ]
     matrices = [(chunks, 4, 128, 128), (128, 512), (128, 256), (128 * ((nz + 1) // 2), 512)]
     coarse, fine_state = pl.pallas_call(
         functools.partial(kernel, sizes),
         out_shape=(
-            jax.ShapeDtypeStruct((5,) + density.shape, F32),
-            jax.ShapeDtypeStruct((5,) + fine, F32),
+            pltpu.VMEM((5,) + density.shape, F32),
+            pltpu.VMEM((5,) + fine, F32),
         ),
         in_specs=[hbm] * 8,
-        out_specs=(hbm, hbm),
+        out_specs=(vmem, vmem),
         scratch_shapes=[pltpu.VMEM(shape, F32) for shape in scratch]
         + [pltpu.VMEM(shape, BF16) for shape in matrices]
         + [pltpu.SMEM((2 * nz,), jnp.int32)] * 2
-        + [pltpu.SemaphoreType.DMA((10,)), pltpu.SemaphoreType.DMA((copies,)), pltpu.SemaphoreType.DMA((copies,))],
+        + [pltpu.SemaphoreType.DMA((8,)), pltpu.SemaphoreType.DMA((copies,)), pltpu.SemaphoreType.DMA((copies,))],
         compiler_params=pltpu.CompilerParams(
             collective_id=0, has_side_effects=True, vmem_limit_bytes=56 * 1024 * 1024
         ),
@@ -604,10 +649,9 @@
             jax.ShapeDtypeStruct(coarse.shape, F32),
             jax.ShapeDtypeStruct(fine_state.shape, F32),
         ),
-        in_specs=[hbm, hbm],
+        in_specs=[vmem, vmem],
         out_specs=(hbm, hbm),
         scratch_shapes=[pltpu.SemaphoreType.DMA((2,))],
-        compiler_params=pltpu.CompilerParams(vmem_limit_bytes=56 * 1024 * 1024),
     )(coarse, fine_state)
     return coarse, fine_state.reshape((5, 1, 1) + fine)
 

time: 30 us -> 28 us (0.933)
  Pallas kernels: 29.2 us -> 25.9 us
  local copies, waits for them, and re-layouts: 0 us -> 1.21 us
    pallas_call x1, Pallas kernels: 3.6 us -> 1.44 us  [on_device(): pl.pallas_call(hand_over, out_shape=(jax.ShapeDtypeStruct(coarse.shape, F...]
    unnamed x0 -> x4, local copies, waits for them, and re-layouts: none -> 1.21 us
    pallas_call x1, Pallas kernels: 25.6 us -> 24.4 us  [on_device(): pl.pallas_call(functools.partial(kernel, sizes), out_shape=(pltpu.VMEM((5...]
where the time goes in v2:
time: 28 us; the launch traced here: 27.7 us
  Pallas kernels  25.9 us (92%)
  local copies, waits for them, and re-layouts  1.21 us (4%)
  between operations  0.65 us (2%)
    pallas_call x1, Pallas kernels, on_device(): pl.pallas_call(functools.partial(kernel, sizes), out_shape=(pltpu.VMEM((5...  24.4 us
    pallas_call x1, Pallas kernels, on_device(): pl.pallas_call(hand_over, out_shape=(jax.ShapeDtypeStruct(coarse.shape, F...  1.44 us
    unnamed x4, local copies, waits for them, and re-layouts  1.21 us

profile of v2, /device:TPU:0, one launch (start us, length us, event | category | flops | bytes accessed | tf_op | source)
XLA Modules:
  0.0 27.7 jit_solution(2702406818309826057)
XLA Ops:
  0.6 24.4 %shard_map.95 = (f32[5,4,4,128]{3,2,1,0:T(4,128)S(1)}, f32[5,2,8,128]{3,2,1,0:T(8,128)S(1)}) custom-call(f32[4,4,128]{2,1,0:T(4,128)} %density_in.1, f32[3,4,4,128]{3,2,1,0:T(4,128)} %velocity_in.1, f32[4,4,128]{2,1,0:T(4,128)} %pressure_in.1, f32[2,8,128]{2,1,0:T(8,128)} %bitcast.9, f32[3,2,8,128]{3,2,1,0:T(8,128)} %bitcast.8, f32[2,8,128]{2,1,0:T(8,128)} %bitcast.10, ...), custom_call_target="tpu_custom_call" | custom-call | tf_op jit(solution)/shard_map/pallas_call | solution.py:621
  25.0 0.0 copy-start
  25.1 0.6 %copy-done = f32[5,4,4,128]{3,2,1,0:T(4,128)} copy-done((f32[5,4,4,128]{3,2,1,0:T(4,128)}, f32[5,4,4,128]{3,2,1,0:T(4,128)S(1)}, u32[]{:S(2)}) %copy-start) | copy-done | bytes 40984
  25.7 0.0 copy-start.1
  25.7 0.6 %copy-done.1 = f32[5,2,8,128]{3,2,1,0:T(8,128)} copy-done((f32[5,2,8,128]{3,2,1,0:T(8,128)}, f32[5,2,8,128]{3,2,1,0:T(8,128)S(1)}, u32[]{:S(2)}) %copy-start.1) | copy-done | bytes 40984
  26.3 1.4 %shard_map.96 = (f32[5,4,4,128]{3,2,1,0:T(4,128)}, f32[5,2,8,128]{3,2,1,0:T(8,128)}) custom-call(f32[5,4,4,128]{3,2,1,0:T(4,128)} %copy-done, f32[5,2,8,128]{3,2,1,0:T(8,128)} %copy-done.1), custom_call_target="tpu_custom_call" | custom-call | tf_op jit(solution)/shard_map/pallas_call | solution.py:646
Async XLA Ops:
  25.0 0.6 %copy-start = (f32[5,4,4,128]{3,2,1,0:T(4,128)}, f32[5,4,4,128]{3,2,1,0:T(4,128)S(1)}, u32[]{:S(2)}) copy-start(f32[5,4,4,128]{3,2,1,0:T(4,128)S(1)} %get-tuple-element.6.coarse) | copy-start | bytes 122884
  25.7 0.6 %copy-start.1 = (f32[5,2,8,128]{3,2,1,0:T(8,128)}, f32[5,2,8,128]{3,2,1,0:T(8,128)S(1)}, u32[]{:S(2)}) copy-start(f32[5,2,8,128]{3,2,1,0:T(8,128)S(1)} %get-tuple-element.7.fine) | copy-start | bytes 122884

commit v3 on v2

--- a/solution.py
+++ b/solution.py
@@ -227,6 +227,9 @@
     mean_got,
     laid,
     upd,
+    win,
+    rim,
+    now,
     sel,
     expand_t,
     expand_y,
@@ -246,9 +249,8 @@
     z_up, z_dn = {"gz": column[1]}, {"gz": column[nz - 1]}
     started = []
 
-    def send(src, dst, device):
-        at = len(started)
-        copy = pltpu.make_async_remote_copy(
+    def remote(src, dst, device, at):
+        return pltpu.make_async_remote_copy(
             src_ref=src,
             dst_ref=dst,
             send_sem=send_sem.at[at],
@@ -256,9 +258,34 @@
             device_id=device,
             device_id_type=MESH,
         )
-        copy.start()
+
+    def planned(src, dst, device):
+        copy = remote(src, dst, device, 12 + len(started))
         started.append(copy)
         return copy
+
+    def halo_copies(at):
+        pairs = [
+            (xs.at[at, 1], xr.at[at, 0], x_up),
+            (xs.at[at, 0], xr.at[at, 1], x_dn),
+            (ys.at[at, 1], yr.at[at, 0], y_up),
+            (ys.at[at, 0], yr.at[at, 1], y_dn),
+            (zs.at[at], zr.at[at, 0], z_up),
+            (zs.at[at], zr.at[at, 1], z_dn),
+        ]
+        return [remote(*pair, 6 * at + k) for k, pair in enumerate(pairs)]
+
+    def to_column(out, into):
+        return [planned(out.at[d - 1], into.at[d], {"gz": column[d]}) for d in range(1, nz)]
+
+    windows, near, far = to_column(msg, got), to_column(msg_z, got_z), to_column(msg_f, got_f)
+    faces_sent = [
+        planned(xs1.at[1], xr1.at[0], x_up),
+        planned(xs1.at[0], xr1.at[1], x_dn),
+        planned(ys1.at[1], yr1.at[0], y_up),
+        planned(ys1.at[0], yr1.at[1], y_dn),
+    ]
+    means_sent = [planned(mean, mean_got.at[d], {"gz": column[d]}) for d in range(1, nz)]
 
     loads = []
     for src, dst in (
@@ -298,16 +325,11 @@
             ys[at, 1, f] = fields[f][2:4, 2:6, :]
         if at == 0:
             pl.semaphore_wait(barrier, len(partners))
-        return [
-            send(xs.at[at, 1], xr.at[at, 0], x_up),
-            send(xs.at[at, 0], xr.at[at, 1], x_dn),
-            send(ys.at[at, 1], yr.at[at, 0], y_up),
-            send(ys.at[at, 0], yr.at[at, 1], y_dn),
-            send(zs.at[at], zr.at[at, 0], z_up),
-            send(zs.at[at], zr.at[at, 1], z_dn),
-        ]
-
-    def coarse_stage(at, copies):
+        for copy in halo_copies(at):
+            copy.start()
+
+    def coarse_stage(at):
+        copies = halo_copies(at)
         for copy in copies[2:6]:
             copy.wait_recv()
         for f in range(5):
@@ -327,8 +349,7 @@
 
     group = lax.broadcasted_iota(jnp.int32, (48, 128), 1) // 32
 
-    def start_picked(rows, size, out, into):
-        copies = []
+    def start_picked(rows, size, out, into, copies):
         for chunk in range((nz + 3) // 4):
             picked = [mm(rows[r], sel[chunk, r]) for r in range(4)]
             for d in range(4 * chunk, min(4 * chunk + 4, nz)):
@@ -346,8 +367,7 @@
                     else:
                         out[d - 1, low:high, :] = part
                 if d > 0:
-                    copies.append(send(out.at[d - 1], into.at[d], {"gz": column[d]}))
-        return copies
+                    copies[d - 1].start()
 
     def take_picked(copies, into):
         for copy in copies:
@@ -405,7 +425,7 @@
         for k in range(3):
             ext[1 + k, 2 + y, 2:6, :] = velocity[k, :, y, :]
         ext[4, 2 + y, 2:6, :] = pressure[:, y, :]
-    halos = start_halos([ext[f, 2:6] for f in range(5)], 0)
+    start_halos([ext[f, 2:6] for f in range(5)], 0)
     for load in loads[3:8]:
         load.wait()
 
@@ -456,82 +476,115 @@
     covered = count[0:4] > 0.0
     share = 1.0 / jnp.maximum(count[0:4], 1.0)
 
-    block, change = coarse_stage(0, halos)
-    start = to_conserved(block)
-    section = [a + DT_COARSE * b for a, b in zip(start, change)]
-    section = to_primitive(section)
-    halos = start_halos(section, 1)
-    for f in range(5):
-        yf[f, 0:4, :] = ext[f, 1, 2:6, :]
-        yf[f, 4:8, :] = ext[f, 6, 2:6, :]
-    rows = []
-    for r in range(4):
-        rows.append(jnp.concatenate([ext[f, 2 + r] for f in range(5)] + [yf[r], yf[4], yf[4]]))
-    windows = start_picked(rows, 48, msg, got)
-    for f in range(5):
-        ext[f, 2:6, 2:6, :] = section[f][:, 2:6, :]
-
-    block, change = coarse_stage(1, halos)
-    section = to_conserved(block)
-    for f in range(5):
-        new = 0.5 * start[f] + 0.5 * (section[f] + DT_COARSE * change[f])
-        upd[f] = new
-        xs1[0, f] = new[:, 2:3, :]
-        xs1[1, f] = new[:, 5:6, :]
-        ys1[0, f] = new[0, 2:6, :]
-        ys1[1, f] = new[3, 2:6, :]
-    faces_sent = [
-        send(xs1.at[1], xr1.at[0], x_up),
-        send(xs1.at[0], xr1.at[1], x_dn),
-        send(ys1.at[1], yr1.at[0], y_up),
-        send(ys1.at[0], yr1.at[1], y_dn),
-    ]
+    @pl.loop(0, 2)
+    def _(at):
+        block, change = coarse_stage(at)
+        base = to_conserved(block)
+        moved = [a + DT_COARSE * b for a, b in zip(base, change)]
+
+        @pl.when(at == 0)
+        def _():
+            section = to_primitive(moved)
+            start_halos(section, 1)
+            for f in range(5):
+                upd[f] = base[f]
+                yf[f, 0:4, :] = ext[f, 1, 2:6, :]
+                yf[f, 4:8, :] = ext[f, 6, 2:6, :]
+            rows = []
+            for r in range(4):
+                rows.append(
+                    jnp.concatenate([ext[f, 2 + r] for f in range(5)] + [yf[r], yf[4], yf[4]])
+                )
+            start_picked(rows, 48, msg, got, windows)
+            for f in range(5):
+                ext[f, 2:6, 2:6, :] = section[f][:, 2:6, :]
+
+        @pl.when(at == 1)
+        def _():
+            for f in range(5):
+                new = 0.5 * upd[f] + 0.5 * moved[f]
+                upd[f] = new
+                xs1[0, f] = new[:, 2:3, :]
+                xs1[1, f] = new[:, 5:6, :]
+                ys1[0, f] = new[0, 2:6, :]
+                ys1[1, f] = new[3, 2:6, :]
+            for copy in faces_sent:
+                copy.start()
 
     rows = []
     for r in range(4):
         rows.append(jnp.concatenate([upd[f, r] for f in range(5)] + [upd[4, r]]))
-    near = start_picked(rows, 40, msg_z, got_z)
+    start_picked(rows, 40, msg_z, got_z, near)
 
     total = take_picked(windows, got)
-    old_inner, old_faces = tiles(total, 5), turned(total[40:48], total[48:56])
-    cells, ghosts = injected(old_inner, old_faces)
-    detail = [fine_density[...]] + [fine_velocity[k] for k in range(3)] + [fine_pressure[...]]
-    prim = [a + b for a, b in zip(cells, detail)]
-    state = to_conserved(prim)
-    rate = fine_tendency(prim, ghosts)
-    stage = [a + DT_FINE * b for a, b in zip(state, rate)]
-
-    for copy in faces_sent:
-        copy.wait_recv()
-    xf[...] = jnp.zeros(xf.shape, F32)
-    for f in range(5):
-        xf[:, f, :] = xr1[0, f, :, 0, :]
-        xf[:, 8 + f, :] = xr1[1, f, :, 0, :]
-        yf[f, 0:4, :] = yr1[0, f]
-        yf[f, 4:8, :] = yr1[1, f]
-    rows = [jnp.concatenate([xf[r], yf[r], yf[4]]) for r in range(4)]
-    far = start_picked(rows, 24, msg_f, got_f)
-
-    rate = fine_tendency(to_primitive(stage), ghosts)
-    state = [0.5 * a + 0.5 * (b + DT_FINE * c) for a, b, c in zip(state, stage, rate)]
-
-    new_inner = tiles(take_picked(near, got_z), 5)
-    total = take_picked(far, got_f)
-    for f in range(5):
-        side = jnp.where(row2 == 1, total[f : f + 1], total[8 + f : 9 + f])
-        new_inner[f] = jnp.where((row2 >= 2) & (row2 < 6), new_inner[f], side)
-    new_faces = turned(total[16:24], total[24:32])
+    for f, tile in enumerate(tiles(total, 5) + turned(total[40:48], total[48:56])):
+        win[f] = tile
 
     def middle(old, new):
         mixed = [0.5 * (a + b) for a, b in zip(to_conserved(old), new)]
         mixed[0] = jnp.where(mixed[0] == 0.0, 1.0, mixed[0])
         return to_primitive(mixed)
 
-    _, ghosts = injected(middle(old_inner, new_inner), middle(old_faces, new_faces))
-    rate = fine_tendency(to_primitive(state), ghosts)
-    stage = [a + DT_FINE * b for a, b in zip(state, rate)]
-    rate = fine_tendency(to_primitive(stage), ghosts)
-    state = [0.5 * a + 0.5 * (b + DT_FINE * c) for a, b, c in zip(state, stage, rate)]
+    @pl.loop(0, 4)
+    def _(step):
+        @pl.when(step % 2 == 0)
+        def _():
+            cells, ghosts = injected([win[f] for f in range(5)], [win[5 + f] for f in range(5)])
+            for axis in range(3):
+                for f in range(5):
+                    rim[axis, f] = ghosts[axis][f]
+
+            @pl.when(step == 0)
+            def _():
+                detail = [fine_density[...]] + [fine_velocity[k] for k in range(3)]
+                detail.append(fine_pressure[...])
+                first = to_conserved([a + b for a, b in zip(cells, detail)])
+                for f in range(5):
+                    fine_out[f] = first[f]
+                    now[f] = first[f]
+
+        current = [now[f] for f in range(5)]
+        ghosts = [[rim[axis, f] for f in range(5)] for axis in range(3)]
+        rate = fine_tendency(to_primitive(current), ghosts)
+        kept = jnp.where(step % 2 == 0, 0.0, 0.5)
+        state = [
+            kept * fine_out[f] + (1.0 - kept) * (current[f] + DT_FINE * rate[f]) for f in range(5)
+        ]
+        for f in range(5):
+            now[f] = state[f]
+
+        @pl.when(step % 2 == 1)
+        def _():
+            for f in range(5):
+                fine_out[f] = state[f]
+
+        @pl.when(step == 0)
+        def _():
+            for copy in faces_sent:
+                copy.wait_recv()
+            xf[...] = jnp.zeros(xf.shape, F32)
+            for f in range(5):
+                xf[:, f, :] = xr1[0, f, :, 0, :]
+                xf[:, 8 + f, :] = xr1[1, f, :, 0, :]
+                yf[f, 0:4, :] = yr1[0, f]
+                yf[f, 4:8, :] = yr1[1, f]
+            rows = [jnp.concatenate([xf[r], yf[r], yf[4]]) for r in range(4)]
+            start_picked(rows, 24, msg_f, got_f, far)
+
+        @pl.when(step == 1)
+        def _():
+            new_inner = tiles(take_picked(near, got_z), 5)
+            total = take_picked(far, got_f)
+            for f in range(5):
+                side = jnp.where(row2 == 1, total[f : f + 1], total[8 + f : 9 + f])
+                new_inner[f] = jnp.where((row2 >= 2) & (row2 < 6), new_inner[f], side)
+            inner = middle([win[f] for f in range(5)], new_inner)
+            sides = middle([win[5 + f] for f in range(5)], turned(total[16:24], total[24:32]))
+            for f in range(5):
+                win[f] = inner[f]
+                win[5 + f] = sides[f]
+
+    state = [now[f] for f in range(5)]
 
     child = big_row // 32 * 8 + (big_row % 16) // 2
     matrix = jnp.where(big_lane == child, 0.125, 0.0).astype(BF16)
@@ -544,10 +597,9 @@
     packed = jnp.concatenate([parts[0] + roll(parts[1], 64, 1) + odd, parts[4]])
     mean[...] = packed
     mean_got[0] = packed
-    copies = [send(mean, mean_got.at[d], {"gz": column[d]}) for d in range(1, nz)]
-    for f in range(5):
-        fine_out[f] = state[f]
-    for copy in copies:
+    for copy in means_sent:
+        copy.start()
+    for copy in means_sent:
         copy.wait_recv()
     rows = []
     for pair in range((nz + 1) // 2):
@@ -566,17 +618,8 @@
         for y in range(4):
             value = laid[tile, y, pl.ds(at, 4, stride=2), :] * share
             coarse_out[f, :, y, :] = jnp.where(covered, value, upd[f, y, 2:6, :])
-    for copy in started:
+    for copy in halo_copies(0) + halo_copies(1) + started:
         copy.wait_send()
-
-
-def hand_over(coarse, fine, coarse_out, fine_out, sems):
-    first = pltpu.make_async_copy(coarse, coarse_out, sems.at[0])
-    second = pltpu.make_async_copy(fine, fine_out, sems.at[1])
-    first.start()
-    second.start()
-    first.wait()
-    second.wait()
 
 
 def on_device(sizes, density, velocity, pressure, fine_density, fine_velocity, fine_pressure, parent, shift):
@@ -616,6 +659,9 @@
         (nz, 16, 128),
         (3, 4, 8, 128),
         (5, 4, 8, 128),
+        (10, 8, 128),
+        (3, 5) + fine,
+        (5,) + fine,
     ]
     matrices = [(chunks, 4, 128, 128), (128, 512), (128, 256), (128 * ((nz + 1) // 2), 512)]
     coarse, fine_state = pl.pallas_call(
@@ -643,16 +689,6 @@
         parent.reshape(-1),
         shift.reshape(-1),
     )
-    coarse, fine_state = pl.pallas_call(
-        hand_over,
-        out_shape=(
-            jax.ShapeDtypeStruct(coarse.shape, F32),
-            jax.ShapeDtypeStruct(fine_state.shape, F32),
-        ),
-        in_specs=[vmem, vmem],
-        out_specs=(hbm, hbm),
-        scratch_shapes=[pltpu.SemaphoreType.DMA((2,))],
-    )(coarse, fine_state)
     return coarse, fine_state.reshape((5, 1, 1) + fine)
 
 

time: 28 us -> 26.7 us (0.954)
  Pallas kernels: 25.9 us -> 24.6 us
    pallas_call x1 -> x0, Pallas kernels: 1.44 us -> none  [on_device(): pl.pallas_call(hand_over, out_shape=(jax.ShapeDtypeStruct(coarse.shape, F...]
    unnamed x4 -> x2, local copies, waits for them, and re-layouts: 1.21 us -> 1.24 us
where the time goes in v3:
time: 26.7 us; the launch traced here: 26.5 us
  Pallas kernels  24.6 us (92%)
  local copies, waits for them, and re-layouts  1.24 us (5%)
  between operations  0.64 us (2%)
    pallas_call x1, Pallas kernels, on_device(): pl.pallas_call(functools.partial(kernel, sizes), out_shape=(pltpu.VMEM((5...  24.6 us
    unnamed x2, local copies, waits for them, and re-layouts  1.24 us

profile of v3, /device:TPU:0, one launch (start us, length us, event | category | flops | bytes accessed | tf_op | source)
XLA Modules:
  0.0 26.5 jit_solution(2591640481804771142)
XLA Ops:
  0.6 24.6 %shard_map.95 = (f32[5,4,4,128]{3,2,1,0:T(4,128)S(1)}, f32[5,2,8,128]{3,2,1,0:T(8,128)S(1)}) custom-call(f32[4,4,128]{2,1,0:T(4,128)} %density_in.1, f32[3,4,4,128]{3,2,1,0:T(4,128)} %velocity_in.1, f32[4,4,128]{2,1,0:T(4,128)} %pressure_in.1, f32[2,8,128]{2,1,0:T(8,128)} %bitcast.10, f32[3,2,8,128]{3,2,1,0:T(8,128)} %bitcast.9, f32[2,8,128]{2,1,0:T(8,128)} %bitcast.11, ...), custom_call_target="tpu_custom_call" | custom-call | tf_op jit(solution)/shard_map/pallas_call | solution.py:667
  25.3 0.6 %copy.13 = f32[5,4,4,128]{3,2,1,0:T(4,128)} copy(f32[5,4,4,128]{3,2,1,0:T(4,128)S(1)} %get-tuple-element.8) | data formatting | bytes 81920
  25.9 0.6 %copy.14 = f32[5,1,1,2,8,128]{5,4,3,2,1,0:T(8,128)} copy(f32[5,1,1,2,8,128]{5,4,3,2,1,0:T(8,128)S(1)} %bitcast.8) | data formatting | bytes 81920

commit v4 on v3

--- a/solution.py
+++ b/solution.py
@@ -10,6 +10,7 @@
 GAMMA = 1.4
 DT_COARSE = 0.05
 DT_FINE = 0.025
+TINY = 1e-30
 MESH = pl.DeviceIdType.MESH
 F32 = jnp.float32
 BF16 = jnp.bfloat16
@@ -25,6 +26,11 @@
     return (out[0:size] + out[size : 2 * size]) + out[2 * size : 3 * size]
 
 
+def inverse(a):
+    near = pl.reciprocal(a, approx=True)
+    return near * (2.0 - a * near)
+
+
 def to_conserved(q):
     rho, u, v, w, p = q
     energy = p * (1.0 / (GAMMA - 1.0)) + 0.5 * rho * (u * u + v * v + w * w)
@@ -33,7 +39,7 @@
 
 def to_primitive(c):
     rho, mx, my, mz, energy = c
-    inv = 1.0 / rho
+    inv = inverse(rho)
     u, v, w = mx * inv, my * inv, mz * inv
     p = (GAMMA - 1.0) * (energy - 0.5 * (mx * u + my * v + mz * w))
     return [rho, u, v, w, p]
@@ -46,19 +52,21 @@
 def hllc(left, right):
     rl, ul, _, _, pl_ = left
     rr, ur, _, _, pr = right
-    cl = jnp.sqrt(GAMMA * pl_ / rl)
-    cr = jnp.sqrt(GAMMA * pr / rr)
+    sound_l = GAMMA * pl_ * inverse(rl)
+    sound_r = GAMMA * pr * inverse(rr)
+    cl = sound_l * lax.rsqrt(jnp.maximum(sound_l, TINY))
+    cr = sound_r * lax.rsqrt(jnp.maximum(sound_r, TINY))
     sl = jnp.minimum(ul - cl, ur - cr)
     sr = jnp.maximum(ul + cl, ur + cr)
     ml = rl * (sl - ul)
     mr = rr * (sr - ur)
-    contact = (pr - pl_ + ml * ul - mr * ur) / (ml - mr)
+    contact = (pr - pl_ + ml * ul - mr * ur) * inverse(ml - mr)
     use_left = (sl >= 0.0) | (contact >= 0.0)
     rho, un, t1, t2, p = [jnp.where(use_left, a, b) for a, b in zip(left, right)]
     wave = jnp.where(use_left, sl, sr)
     mass = jnp.where(use_left, ml, mr)
     outside = (sl >= 0.0) | (jnp.logical_not(use_left) & (sr < 0.0))
-    scale = 1.0 / (wave - contact)
+    scale = inverse(wave - contact)
     energy = p * (1.0 / (GAMMA - 1.0)) + 0.5 * rho * (un * un + t1 * t1 + t2 * t2)
     star_rho = mass * scale
     star_energy = ((wave - un) * energy + (contact - un) * (mass * contact + p)) * scale
@@ -391,31 +399,31 @@
             out = jnp.where(row2 >= 2 * k, tile[base + k : base + k + 1], out)
         return jnp.broadcast_to(out, (8, 128))
 
-    def injected(inner, faces):
-        rows = [doubled(tile, 2) for tile in inner] + list(inner)
-        wide = mm(jnp.concatenate(rows), expand_t[...])
+    def both(matrix, first_row, left):
+        rows = matrix[first_row : first_row + 8]
+        return jnp.stack([rows[:, left : left + 128], rows[:, left + 128 : left + 256]])
+
+    def x_rows(inner):
+        out = []
+        for at in (1, 6):
+            tile = jnp.zeros((8, 128), F32)
+            for f in range(5):
+                tile = jnp.where(row2 == f, inner[f][at : at + 1], tile)
+            out.append(tile)
+        return out
+
+    def put_x(matrix, first_row):
+        low, high = both(matrix, first_row, 0), both(matrix, first_row + 8, 0)
+        for f in range(5):
+            rim[0, f] = jnp.where(row3 < 4, low[:, f : f + 1, :], high[:, f : f + 1, :])
+
+    def put_y(faces):
         rows = [doubled(tile, 0) for tile in faces] + [doubled(tile, 4) for tile in faces]
         sides = mm(jnp.concatenate(rows), expand_y[...])
-
-        def both(matrix, first_row, left, right):
-            return jnp.stack(
-                [
-                    matrix[first_row : first_row + 8, left : left + 128],
-                    matrix[first_row : first_row + 8, right : right + 128],
-                ]
-            )
-
-        row = lax.broadcasted_iota(jnp.int32, (1, 8, 128), 1)
-        cells, in_x, in_y, in_z = [], [], [], []
-        for f in range(5):
-            cells.append(both(wide, 8 * f, 0, 128))
-            in_z.append(both(wide, 8 * f, 256, 384))
-            edge = both(wide, 40 + 8 * f, 0, 128)
-            in_x.append(jnp.where(row < 4, edge[:, 1:2, :], edge[:, 6:7, :]))
-            low = both(sides, 8 * f, 0, 128)
-            high = both(sides, 40 + 8 * f, 0, 128)
-            in_y.append(jnp.where(lane3 < 64, low, high))
-        return cells, (in_x, in_y, in_z)
+        for f in range(5):
+            rim[1, f] = jnp.where(lane3 < 64, both(sides, 8 * f, 0), both(sides, 40 + 8 * f, 0))
+
+    row3 = lax.broadcasted_iota(jnp.int32, (1, 8, 128), 1)
 
     ext[...] = jnp.ones(ext.shape, F32)
     for load in loads[0:3]:
@@ -517,8 +525,31 @@
     start_picked(rows, 40, msg_z, got_z, near)
 
     total = take_picked(windows, got)
-    for f, tile in enumerate(tiles(total, 5) + turned(total[40:48], total[48:56])):
-        win[f] = tile
+    old_inner, old_faces = tiles(total, 5), turned(total[40:48], total[48:56])
+    for f in range(5):
+        win[f] = old_inner[f]
+        win[5 + f] = old_faces[f]
+    rows = [doubled(tile, 2) for tile in old_inner] + x_rows(old_inner)
+    wide = mm(jnp.concatenate(rows + rows[0:1]), expand_t[...])
+    detail = [fine_density[...]] + [fine_velocity[k] for k in range(3)] + [fine_pressure[...]]
+    first = to_conserved([both(wide, 8 * f, 0) + detail[f] for f in range(5)])
+    for f in range(5):
+        fine_out[f] = first[f]
+        now[f] = first[f]
+        rim[2, f] = both(wide, 8 * f, 256)
+    put_x(wide, 40)
+    put_y(old_faces)
+
+    for copy in faces_sent:
+        copy.wait_recv()
+    xf[...] = jnp.zeros(xf.shape, F32)
+    for f in range(5):
+        xf[:, f, :] = xr1[0, f, :, 0, :]
+        xf[:, 8 + f, :] = xr1[1, f, :, 0, :]
+        yf[f, 0:4, :] = yr1[0, f]
+        yf[f, 4:8, :] = yr1[1, f]
+    rows = [jnp.concatenate([xf[r], yf[r], yf[4]]) for r in range(4)]
+    start_picked(rows, 24, msg_f, got_f, far)
 
     def middle(old, new):
         mixed = [0.5 * (a + b) for a, b in zip(to_conserved(old), new)]
@@ -527,22 +558,6 @@
 
     @pl.loop(0, 4)
     def _(step):
-        @pl.when(step % 2 == 0)
-        def _():
-            cells, ghosts = injected([win[f] for f in range(5)], [win[5 + f] for f in range(5)])
-            for axis in range(3):
-                for f in range(5):
-                    rim[axis, f] = ghosts[axis][f]
-
-            @pl.when(step == 0)
-            def _():
-                detail = [fine_density[...]] + [fine_velocity[k] for k in range(3)]
-                detail.append(fine_pressure[...])
-                first = to_conserved([a + b for a, b in zip(cells, detail)])
-                for f in range(5):
-                    fine_out[f] = first[f]
-                    now[f] = first[f]
-
         current = [now[f] for f in range(5)]
         ghosts = [[rim[axis, f] for f in range(5)] for axis in range(3)]
         rate = fine_tendency(to_primitive(current), ghosts)
@@ -560,29 +575,23 @@
 
         @pl.when(step == 0)
         def _():
-            for copy in faces_sent:
-                copy.wait_recv()
-            xf[...] = jnp.zeros(xf.shape, F32)
+            inner = middle([win[f] for f in range(5)], tiles(take_picked(near, got_z), 5))
+            rows = [doubled(tile, 2) for tile in inner]
+            wide = mm(jnp.concatenate(rows + rows[0:1]), expand_t[:, 256:512])
             for f in range(5):
-                xf[:, f, :] = xr1[0, f, :, 0, :]
-                xf[:, 8 + f, :] = xr1[1, f, :, 0, :]
-                yf[f, 0:4, :] = yr1[0, f]
-                yf[f, 4:8, :] = yr1[1, f]
-            rows = [jnp.concatenate([xf[r], yf[r], yf[4]]) for r in range(4)]
-            start_picked(rows, 24, msg_f, got_f, far)
+                rim[3, f] = both(wide, 8 * f, 0)
 
         @pl.when(step == 1)
         def _():
-            new_inner = tiles(take_picked(near, got_z), 5)
             total = take_picked(far, got_f)
+            put_y(middle([win[5 + f] for f in range(5)], turned(total[16:24], total[24:32])))
+            sides = [
+                jnp.where(row2 == 1, total[f : f + 1], total[8 + f : 9 + f]) for f in range(5)
+            ]
+            rows = x_rows(middle([win[f] for f in range(5)], sides))
+            put_x(mm(jnp.concatenate(rows), expand_t[:, 0:256]), 0)
             for f in range(5):
-                side = jnp.where(row2 == 1, total[f : f + 1], total[8 + f : 9 + f])
-                new_inner[f] = jnp.where((row2 >= 2) & (row2 < 6), new_inner[f], side)
-            inner = middle([win[f] for f in range(5)], new_inner)
-            sides = middle([win[5 + f] for f in range(5)], turned(total[16:24], total[24:32]))
-            for f in range(5):
-                win[f] = inner[f]
-                win[5 + f] = sides[f]
+                rim[2, f] = rim[3, f]
 
     state = [now[f] for f in range(5)]
 
@@ -660,7 +669,7 @@
         (3, 4, 8, 128),
         (5, 4, 8, 128),
         (10, 8, 128),
-        (3, 5) + fine,
+        (4, 5) + fine,
         (5,) + fine,
     ]
     matrices = [(chunks, 4, 128, 128), (128, 512), (128, 256), (128 * ((nz + 1) // 2), 512)]

time: 26.7 us -> 26.7 us (level)
  no operation moved by 1% of the time
where the time goes in v4:
time: 26.7 us; the launch traced here: 26.5 us
  Pallas kernels  24.6 us (92%)
  local copies, waits for them, and re-layouts  1.24 us (5%)
  between operations  0.64 us (2%)
    pallas_call x1, Pallas kernels, on_device(): pl.pallas_call(functools.partial(kernel, sizes), out_shape=(pltpu.VMEM((5...  24.6 us
    unnamed x2, local copies, waits for them, and re-layouts  1.24 us

profile of v4, /device:TPU:0, one launch (start us, length us, event | category | flops | bytes accessed | tf_op | source)
XLA Modules:
  0.0 26.5 jit_solution(15908114409061396362)
XLA Ops:
  0.6 24.6 %shard_map.95 = (f32[5,4,4,128]{3,2,1,0:T(4,128)S(1)}, f32[5,2,8,128]{3,2,1,0:T(8,128)S(1)}) custom-call(f32[4,4,128]{2,1,0:T(4,128)} %density_in.1, f32[3,4,4,128]{3,2,1,0:T(4,128)} %velocity_in.1, f32[4,4,128]{2,1,0:T(4,128)} %pressure_in.1, f32[2,8,128]{2,1,0:T(8,128)} %bitcast.10, f32[3,2,8,128]{3,2,1,0:T(8,128)} %bitcast.9, f32[2,8,128]{2,1,0:T(8,128)} %bitcast.11, ...), custom_call_target="tpu_custom_call" | custom-call | tf_op jit(solution)/shard_map/pallas_call | solution.py:676
  25.2 0.6 %copy.13 = f32[5,4,4,128]{3,2,1,0:T(4,128)} copy(f32[5,4,4,128]{3,2,1,0:T(4,128)S(1)} %get-tuple-element.8) | data formatting | bytes 81920
  25.9 0.6 %copy.14 = f32[5,1,1,2,8,128]{5,4,3,2,1,0:T(8,128)} copy(f32[5,1,1,2,8,128]{5,4,3,2,1,0:T(8,128)S(1)} %bitcast.8) | data formatting | bytes 81920

commit v5 on v4

--- a/solution.py
+++ b/solution.py
@@ -327,10 +327,12 @@
     def start_halos(fields, at):
         pack_z(fields, at)
         for f in range(5):
-            xs[at, 0, f] = fields[f][:, 2:4, :]
-            xs[at, 1, f] = fields[f][:, 4:6, :]
-            ys[at, 0, f] = fields[f][0:2, 2:6, :]
-            ys[at, 1, f] = fields[f][2:4, 2:6, :]
+            for y in range(4):
+                xs[at, 0, f, 2 * y : 2 * y + 2, :] = fields[f][y, 2:4, :]
+                xs[at, 1, f, 2 * y : 2 * y + 2, :] = fields[f][y, 4:6, :]
+            for k in range(2):
+                ys[at, 0, f, 4 * k : 4 * k + 4, :] = fields[f][k, 2:6, :]
+                ys[at, 1, f, 4 * k : 4 * k + 4, :] = fields[f][2 + k, 2:6, :]
         if at == 0:
             pl.semaphore_wait(barrier, len(partners))
         for copy in halo_copies(at):
@@ -341,16 +343,18 @@
         for copy in copies[2:6]:
             copy.wait_recv()
         for f in range(5):
-            ext[f, 0:2, 2:6, :] = yr[at, 0, f]
-            ext[f, 6:8, 2:6, :] = yr[at, 1, f]
+            for k in range(2):
+                ext[f, k, 2:6, :] = yr[at, 0, f, 4 * k : 4 * k + 4, :]
+                ext[f, 6 + k, 2:6, :] = yr[at, 1, f, 4 * k : 4 * k + 4, :]
         ends = jnp.where(lane3 % 4 < 2, zr[at, 0], zr[at, 1])
         ends = [roll(ends, 126 - 4 * f, 2) for f in range(5)]
         change = coarse_fluxes_yz([ext[f] for f in range(5)], ends)
         for copy in copies[0:2]:
             copy.wait_recv()
         for f in range(5):
-            ext[f, 2:6, 0:2, :] = xr[at, 0, f]
-            ext[f, 2:6, 6:8, :] = xr[at, 1, f]
+            for y in range(4):
+                ext[f, 2 + y, 0:2, :] = xr[at, 0, f, 2 * y : 2 * y + 2, :]
+                ext[f, 2 + y, 6:8, :] = xr[at, 1, f, 2 * y : 2 * y + 2, :]
         block = [ext[f, 2:6] for f in range(5)]
         change = [a + b for a, b in zip(change, coarse_fluxes_x(block))]
         return block, change
@@ -512,10 +516,11 @@
             for f in range(5):
                 new = 0.5 * upd[f] + 0.5 * moved[f]
                 upd[f] = new
-                xs1[0, f] = new[:, 2:3, :]
-                xs1[1, f] = new[:, 5:6, :]
-                ys1[0, f] = new[0, 2:6, :]
-                ys1[1, f] = new[3, 2:6, :]
+                for y in range(4):
+                    xs1[0, 4 * f + y : 4 * f + y + 1, :] = new[y, 2:3, :]
+                    xs1[1, 4 * f + y : 4 * f + y + 1, :] = new[y, 5:6, :]
+                ys1[0, 4 * f : 4 * f + 4, :] = new[0, 2:6, :]
+                ys1[1, 4 * f : 4 * f + 4, :] = new[3, 2:6, :]
             for copy in faces_sent:
                 copy.start()
 
@@ -544,10 +549,10 @@
         copy.wait_recv()
     xf[...] = jnp.zeros(xf.shape, F32)
     for f in range(5):
-        xf[:, f, :] = xr1[0, f, :, 0, :]
-        xf[:, 8 + f, :] = xr1[1, f, :, 0, :]
-        yf[f, 0:4, :] = yr1[0, f]
-        yf[f, 4:8, :] = yr1[1, f]
+        xf[:, f, :] = xr1[0, 4 * f : 4 * f + 4, :]
+        xf[:, 8 + f, :] = xr1[1, 4 * f : 4 * f + 4, :]
+        yf[f, 0:4, :] = yr1[0, 4 * f : 4 * f + 4, :]
+        yf[f, 4:8, :] = yr1[1, 4 * f : 4 * f + 4, :]
     rows = [jnp.concatenate([xf[r], yf[r], yf[4]]) for r in range(4)]
     start_picked(rows, 24, msg_f, got_f, far)
 
@@ -646,16 +651,16 @@
         (3,) + fine,
         fine,
         (5, 8, 8, 128),
-        (2, 2, 5, 4, 2, 128),
-        (2, 2, 5, 4, 2, 128),
-        (2, 2, 5, 2, 4, 128),
-        (2, 2, 5, 2, 4, 128),
+        (2, 2, 5, 8, 128),
+        (2, 2, 5, 8, 128),
+        (2, 2, 5, 8, 128),
+        (2, 2, 5, 8, 128),
         (2, 4, 8, 128),
         (2, 2, 4, 8, 128),
-        (2, 5, 4, 1, 128),
-        (2, 5, 4, 1, 128),
-        (2, 5, 4, 128),
-        (2, 5, 4, 128),
+        (2, 20, 128),
+        (2, 20, 128),
+        (2, 20, 128),
+        (2, 20, 128),
         (5, 8, 128),
         (4, 16, 128),
         (nz - 1, 56, 128),

time: 26.7 us -> 26.7 us (level)
  no operation moved by 1% of the time
where the time goes in v5:
time: 26.7 us; the launch traced here: 26.5 us
  Pallas kernels  24.6 us (92%)
  local copies, waits for them, and re-layouts  1.24 us (5%)
  between operations  0.64 us (2%)
    pallas_call x1, Pallas kernels, on_device(): pl.pallas_call(functools.partial(kernel, sizes), out_shape=(pltpu.VMEM((5...  24.6 us
    unnamed x2, local copies, waits for them, and re-layouts  1.24 us

profile of v5, /device:TPU:0, one launch (start us, length us, event | category | flops | bytes accessed | tf_op | source)
XLA Modules:
  0.0 26.5 jit_solution(15795536734236598545)
XLA Ops:
  0.6 24.6 %shard_map.95 = (f32[5,4,4,128]{3,2,1,0:T(4,128)S(1)}, f32[5,2,8,128]{3,2,1,0:T(8,128)S(1)}) custom-call(f32[4,4,128]{2,1,0:T(4,128)} %density_in.1, f32[3,4,4,128]{3,2,1,0:T(4,128)} %velocity_in.1, f32[4,4,128]{2,1,0:T(4,128)} %pressure_in.1, f32[2,8,128]{2,1,0:T(8,128)} %bitcast.10, f32[3,2,8,128]{3,2,1,0:T(8,128)} %bitcast.9, f32[2,8,128]{2,1,0:T(8,128)} %bitcast.11, ...), custom_call_target="tpu_custom_call" | custom-call | tf_op jit(solution)/shard_map/pallas_call | solution.py:681
  25.2 0.6 %copy.13 = f32[5,4,4,128]{3,2,1,0:T(4,128)} copy(f32[5,4,4,128]{3,2,1,0:T(4,128)S(1)} %get-tuple-element.8) | data formatting | bytes 81920
  25.9 0.6 %copy.14 = f32[5,1,1,2,8,128]{5,4,3,2,1,0:T(8,128)} copy(f32[5,1,1,2,8,128]{5,4,3,2,1,0:T(8,128)S(1)} %bitcast.8) | data formatting | bytes 81920
